TPU v7x, 32 devices: a whole 2x2x4 slice. The times are simulated.
32 devices in a mesh: leaf: 2 (over y), row: 4 (over z), col: 4 (over x, core).
Axes of the slice: x: 2, y: 2, z: 4, core: 2. Of those that a mesh axis runs over, the one named last changes fastest.
Arguments:
- child_front: float32 [2, 4096, 4096], P('leaf', 'row', 'col'), may hold values from -2 to 4, as said below
- parent_front: float32 [8192, 8, 8, 128], P('row', None, ('leaf', 'col')), may hold values from -2 to 4, as said below
- block_map: int32 [2, 30], replicated, may hold values from 0 to 63, as said below
Outputs:
- child_factor: float32 [2, 4096, 256], P('leaf', 'row')
- parent_out: float32 [8192, 8, 8, 128], P('row', None, ('leaf', 'col'))
Inputs may be any that keep to these rules, and one draw needn't show every extreme that they name: `child_front`: each child front is symmetric positive definite, with smallest eigenvalue above 0.1. `parent_front`: viewed as a 8192 x 8192 matrix, the parent front is symmetric positive definite, with smallest eigenvalue above 0.1. `block_map`: row c lists, in order, the parent block that receives each of the 30 trailing blocks of child front c; the entries of a row are distinct parent blocks. Put 2 empty blocks in front of a row and cut it into aligned groups of 8: in every group at most 2 entries share the value of entry // 16, and at most 2 share the value of entry modulo 4; both bounds are reached.
All inputs are finite; a program needn't handle non-finite values.
Results may differ from a plain program's by a relative error of at most 0.0001.
Values sent between devices are 32-bit elements; how exact they have to be, the bound alone decides.
A program may use at most 128 MiB of HBM per device.

v0:
```python
import jax
import jax.numpy as jnp
from jax import lax
from jax.sharding import PartitionSpec as P

FP = 8192
PANEL = 256
BLOCK = 128


def spread(value, axis, source):
    kept = jnp.where(lax.axis_index(axis) == source, value, 0).astype(value.dtype)
    return lax.psum(kept, axis)


def matmul(left, right):
    return jnp.dot(left, right, precision=lax.Precision.HIGHEST, preferred_element_type=jnp.float32)


def contract(form, left, right):
    return jnp.einsum(
        form, left, right, precision=lax.Precision.HIGHEST, preferred_element_type=jnp.float32
    )


def lower_inverse(corner):
    lower_factor = jnp.linalg.cholesky(corner)
    identity = jnp.eye(corner.shape[0], dtype=jnp.float32)
    return jax.scipy.linalg.solve_triangular(lower_factor, identity, lower=True)


def slot_ranks(targets, usable):
    count = targets.shape[-1]
    same = (
        (targets[..., :, None] == targets[..., None, :])
        & usable[..., :, None]
        & usable[..., None, :]
    )
    before = jnp.arange(count)[None, :] < jnp.arange(count)[:, None]
    return jnp.sum(same & before, axis=-1)


def pick_send(targets, ranks, usable, count, capacity):
    destination = jnp.arange(count)[:, None, None]
    slot_index = jnp.arange(capacity)[None, :, None]
    chosen = (
        (targets[None, None, :] == destination)
        & (ranks[None, None, :] == slot_index)
        & usable[None, None, :]
    )
    return chosen.astype(jnp.float32)


def column_regroup(
    col_target, col_rank, usable, maps, col_id, capacity, leaves, grid_cols, kblocks, period
):
    leaf_of = maps % period // grid_cols
    slot_of = maps // period
    arrived = (col_target == col_id) & usable
    chosen = arrived[None, None, :, None, :]
    chosen = chosen & (
        col_rank[None, None, :, None, :] == jnp.arange(capacity)[None, None, None, :, None]
    )
    chosen = chosen & (
        leaf_of[None, None, :, None, :] == jnp.arange(leaves)[:, None, None, None, None]
    )
    chosen = chosen & (
        slot_of[None, None, :, None, :] == jnp.arange(kblocks)[None, :, None, None, None]
    )
    return jnp.sum(chosen.astype(jnp.float32), axis=-1)


def per_device(child_front, parent_front, block_map):
    front_local = child_front[0]
    grid_rows = lax.axis_size("row")
    grid_cols = lax.axis_size("col")
    leaves = lax.axis_size("leaf")
    row_id = lax.axis_index("row")
    col_id = lax.axis_index("col")
    leaf_id = lax.axis_index("leaf")
    local_rows = front_local.shape[0]
    child_blocks = local_rows // BLOCK
    capacity = max(1, child_blocks // grid_rows)
    parent_blocks = FP // BLOCK
    per_row = parent_blocks // grid_rows
    period = leaves * grid_cols
    kblocks = parent_blocks // period
    parent_rows = per_row * BLOCK
    lead = PANEL // BLOCK
    top_rows = spread(front_local[:PANEL, :], "row", 0)
    panel_rows, corner = (
        spread(front_local[:, :PANEL], "col", 0),
        spread(top_rows[:, :PANEL], "col", 0),
    )
    inverse = lower_inverse(corner)
    factor = matmul(panel_rows, inverse.T)
    schur = front_local - matmul(factor, matmul(inverse, top_rows))
    padded = jnp.concatenate([jnp.full((leaves, lead), -1, jnp.int32), block_map], axis=1)
    all_maps = padded.reshape(leaves, grid_rows, child_blocks)
    all_usable = all_maps >= 0
    own_maps = lax.dynamic_index_in_dim(all_maps, leaf_id, 0, keepdims=False)
    own_usable = own_maps >= 0
    col_target = jnp.where(own_usable, own_maps % grid_cols, -1)
    col_rank = slot_ranks(col_target, own_usable)
    col_send = pick_send(
        lax.dynamic_index_in_dim(col_target, col_id, 0, keepdims=False),
        lax.dynamic_index_in_dim(col_rank, col_id, 0, keepdims=False),
        lax.dynamic_index_in_dim(own_usable, col_id, 0, keepdims=False),
        grid_cols,
        capacity,
    )
    regroup = column_regroup(
        col_target,
        col_rank,
        own_usable,
        own_maps,
        col_id,
        capacity,
        leaves,
        grid_cols,
        kblocks,
        period,
    )
    column_out = contract("dks,rsb->dkrb", col_send, schur.reshape(local_rows, child_blocks, BLOCK))
    column_in = lax.all_to_all(column_out, "col", split_axis=0, concat_axis=0, tiled=True)
    leaf_out = contract("lmnk,nkrb->lrmb", regroup, column_in)
    leaf_in = lax.all_to_all(leaf_out, "leaf", split_axis=0, concat_axis=0, tiled=True)
    all_target = jnp.where(all_usable, all_maps // per_row, -1)
    all_rank = slot_ranks(all_target, all_usable)
    mine_target = lax.dynamic_index_in_dim(all_target, row_id, 1, keepdims=False)
    mine_rank = lax.dynamic_index_in_dim(all_rank, row_id, 1, keepdims=False)
    mine_usable = lax.dynamic_index_in_dim(all_usable, row_id, 1, keepdims=False)
    row_pick = mine_target[None, :, None, :] == jnp.arange(grid_rows)[:, None, None, None]
    row_pick = row_pick & (mine_rank[None, :, None, :] == jnp.arange(capacity)[None, None, :, None])
    row_pick = (row_pick & mine_usable[None, :, None, :]).astype(jnp.float32)
    row_blocks = leaf_in.reshape(leaves, child_blocks, BLOCK, kblocks, BLOCK)
    row_out = contract("dcks,csbmt->dckbmt", row_pick, row_blocks)
    row_in = lax.all_to_all(row_out, "row", split_axis=0, concat_axis=0, tiled=True)
    placed = ((all_target == row_id) & all_usable)[None, :, :, None, :]
    placed = placed & (
        all_rank[None, :, :, None, :] == jnp.arange(capacity)[None, None, None, :, None]
    )
    placed = placed & (
        (all_maps % per_row)[None, :, :, None, :] == jnp.arange(per_row)[:, None, None, None, None]
    )
    placement = jnp.sum(placed.astype(jnp.float32), axis=-1)
    contribution = contract("pcnk,nckbmt->pbmt", placement, row_in).reshape(
        parent_rows, kblocks, BLOCK
    )
    assembled = parent_front[:, :, 0, :] + contribution
    top_parent = spread(assembled[:PANEL].reshape(PANEL, kblocks * BLOCK), "row", 0)
    top_blocks = top_parent.reshape(PANEL, kblocks, BLOCK)
    pieces = []
    corners = []
    for block_index in range(lead):
        slot_here = block_index // period
        piece, corner_piece = (
            spread(assembled[:, slot_here, :], ("leaf", "col"), block_index % period),
            spread(top_blocks[:, slot_here, :], ("leaf", "col"), block_index % period),
        )
        pieces.append(piece)
        corners.append(corner_piece)
    panel_parent = jnp.concatenate(pieces, axis=1)
    corner_parent = jnp.concatenate(corners, axis=1)
    inverse_parent = lower_inverse(corner_parent)
    parent_factor = matmul(panel_parent, inverse_parent.T)
    upper_parent = matmul(inverse_parent, top_parent)
    updated = assembled - matmul(parent_factor, upper_parent).reshape(parent_rows, kblocks, BLOCK)
    global_row = row_id * parent_rows + jnp.arange(parent_rows)
    device_column = leaf_id * grid_cols + col_id
    global_col = (jnp.arange(kblocks)[:, None] * period + device_column) * BLOCK + jnp.arange(
        BLOCK
    )[None, :]
    panel_values = jnp.take(parent_factor, jnp.minimum(global_col, PANEL - 1), axis=1)
    kept = jnp.where((global_row < PANEL)[:, None, None], assembled, updated)
    result = jnp.where((global_col < PANEL)[None, :, :], panel_values, kept)
    return (factor[None], result[:, :, None, :])


def solution(mesh):
    placed = (P("leaf", "row", "col"), P("row", None, ("leaf", "col"), None), P())
    return jax.shard_map(
        per_device,
        mesh=mesh,
        in_specs=placed,
        out_specs=(P("leaf", "row", None), P("row", None, ("leaf", "col"), None)),
        check_vma=False,
    )
```

profile of v0, /device:TPU:0, one launch (start us, length us, event | category | flops | bytes accessed | tf_op | source)
XLA Modules:
  0.0 859.5 jit_solution(11439584800377646933)
XLA Ops:
  7.2 5.3 copy.74
  12.6 2.3 fusion.22
  15.5 2.3 slice_select_fusion.2
  17.8 51.8 %all-reduce.9.cloned.1.call-done = f32[256,1024]{0,1:T(8,128)} async-done(((f32[256,1024]{0,1:T(8,128)}), f32[256,1024]{0,1:T(8,128)}) %all-reduce.9.cloned.1.call-update) | async-done | bytes 1048592 | tf_op jit(solution)/shard_map/psum | solution.py:13
  69.6 1.8 slice_select_fusion.3
  71.4 39.9 %all-reduce.15.cloned.1.call-done = (f32[1024,256]{0,1:T(8,128)}, f32[256,256]{0,1:T(8,128)}) async-done(((f32[1024,256]{0,1:T(8,128)}, f32[256,256]{0,1:T(8,128)}), (f32[1024,256]{0,1:T(8,128)}, f32[256,256]{0,1:T(8,128)})) %all-reduce.15.cloned.1.call-update) | async-done | bytes 1310736 | tf_op jit(solution)/shard_map/psum | solution.py:13
  111.4 1.1 copy.76
  112.4 1.0 fusion.24
  113.4 11.7 %cholesky.130 = f32[128,128]{1,0:T(8,128)S(1)} custom-call(f32[128,128]{1,0:T(8,128)S(1)} %cholesky.194), custom_call_target="Cholesky" | custom-call | tf_op jit(solution)/shard_map/jit(cholesky)/cholesky | solution.py:27
  125.2 9.8 %custom-call.13 = f32[1,128,128]{1,2,0:T(8,128)S(1)} custom-call(f32[1,128,128]{2,1,0:T(8,128)S(1)} %get-tuple-element.71), custom_call_target="InvertDiagBlocksLowerTriangular" | custom-call | tf_op jit(solution)/shard_map/jit(cholesky)/cholesky | solution.py:27
  135.5 11.7 %cholesky.147 = f32[128,128]{1,0:T(8,128)S(1)} custom-call(f32[128,128]{1,0:T(8,128)S(1)} %convolution_subtract_fusion.4), custom_call_target="Cholesky" | custom-call | tf_op jit(solution)/shard_map/jit(cholesky)/cholesky | solution.py:27
  147.3 0.7 compare_reduce_fusion.2
  149.3 4.1 while.4
  149.5 0.6 fusion.97
  150.1 1.4 bitcast_dynamic-update-slice_fusion.4
  151.5 0.6 fusion.97
  152.1 1.4 bitcast_dynamic-update-slice_fusion.4
  153.4 19.7 %custom-call.14 = f32[2,128,128]{1,2,0:T(8,128)S(1)} custom-call(f32[2,128,128]{2,1,0:T(8,128)S(1)} %get-tuple-element.18), custom_call_target="InvertDiagBlocksLowerTriangular" | custom-call | tf_op jit(solution)/shard_map/jit(_solve_triangular)/triangular_solve | solution.py:29
  174.0 3.4 fusion.28
  177.4 1.0 fusion.27
  178.5 5.3 convolution_subtract_fusion
  183.8 5.5 copy.77
  189.4 9.7 %fusion.10 = f32[4,2,1024,128]{3,1,2,0:T(2,128)} fusion(f32[1024,8,128]{2,1,0:T(8,128)} %copy.77, pred[4,2,8,1]{2,0,1,3:T(4,128)(4,1)S(1)} %and_bitcast_fusion), kind=kOutput, calls=%fused_computation.17 | convolution fusion | flops 100663296 | bytes 8388672 | tf_op jit(solution)/shard_map/dks,rsb->dkrb/dot_general | solution.py:21
  199.1 4.8 all-to-all-start
  204.1 48.0 %all-to-all-done = f32[4,2,1024,128]{3,1,2,0:T(2,128)} async-done(((f32[4,2,1024,128]{3,1,2,0:T(2,128)}), f32[4,2,1024,128]{3,1,2,0:T(2,128)}, u32[]{:S(2)}, u32[]{:S(2)}) %all-to-all-start) | async-done | bytes 4194336 | tf_op jit(solution)/shard_map/all_to_all | solution.py:125
  252.2 12.8 %fusion.12 = f32[2,1024,8,128]{3,2,0,1:T(8,128)S(1)} fusion(f32[2,8,4,2]{1,3,2,0:T(2,128)S(1)} %convert_reduce_fusion, f32[4,2,1024,128]{3,1,2,0:T(2,128)} %all-to-all-done), kind=kOutput, calls=%fused_computation.19 | convolution fusion | flops 201326592 | bytes 12583424 | tf_op jit(solution)/shard_map/lmnk,nkrb->lrmb/dot_general | solution.py:21
  265.0 3.9 copy.80
  269.0 6.9 all-to-all-start.1
  276.3 92.0 %all-to-all-done.1 = f32[2,1024,8,128]{3,2,1,0:T(8,128)} async-done(((f32[2,1024,8,128]{3,2,1,0:T(8,128)}), f32[2,1024,8,128]{3,2,1,0:T(8,128)}, u32[]{:S(2)}, u32[]{:S(2)}) %all-to-all-start.1) | async-done | bytes 8388640 | tf_op jit(solution)/shard_map/all_to_all | solution.py:127
  368.3 14.3 %fusion.5 = f32[4,2,2,128,8,128]{5,0,2,1,4,3:T(4,128)S(1)} fusion(f32[2,8,128,8,128,1]{4,3,2,1,0,5:T(8,128)} %bitcast.23, pred[2,8]{1,0:T(4,128)(4,1)S(1)} %bitcast.179, pred[2,2,8]{2,1,0:T(4,128)(4,1)S(1)} %iota_compare_fusion.9, pred[4,2,8]{2,0,1:T(4,128)(4,1)S(1)} %iota_compare_fusion.6), kind=kOutput, calls=%fused_computation.14 | convolution fusion | flops 201326848 | bytes 16777328 | tf_op jit(solution)/shard_map/dcks,csbmt->dckbmt/dot_general | solution.py:21
  382.6 6.8 copy.82
  389.4 5.6 all-to-all-start.2
  395.4 182.0 %all-to-all-done.2 = f32[4,2,2,128,8,128]{5,2,1,4,3,0:T(2,128)} async-done(((f32[4,2,2,128,8,128]{5,2,1,4,3,0:T(2,128)}), f32[4,2,2,128,8,128]{5,2,1,4,3,0:T(2,128)}, u32[]{:S(2)}, u32[]{:S(2)}) %all-to-all-start.2) | async-done | bytes 8388640 | tf_op jit(solution)/shard_map/all_to_all | solution.py:138
  577.3 20.9 %fusion.15 = f32[16,128,8,128]{3,0,2,1:T(8,128)S(1)} fusion(f32[4,2,2,128,8,128]{5,2,1,4,3,0:T(2,128)} %all-to-all-done.2, f32[16,2,4,2]{0,3,2,1:T(2,128)S(1)} %convert_reduce_fusion.1), kind=kOutput, calls=%fused_computation.20 | convolution fusion | flops 402653184 | bytes 16778240 | tf_op jit(solution)/shard_map/pcnk,nckbmt->pbmt/dot_general | solution.py:21
  598.3 2.7 copy.85
  601.0 6.9 bitcast_add_fusion.1
  607.9 3.4 copy-done.3
  611.4 1.4 copy.111
  613.0 5.4 fusion.77
  618.4 1.0 select_bitcast_fusion
  619.4 43.1 %all-reduce.11.cloned.1.call-done = f32[256,1024]{0,1:T(8,128)} async-done(((f32[256,1024]{0,1:T(8,128)}), f32[256,1024]{0,1:T(8,128)}) %all-reduce.11.cloned.1.call-update) | async-done | bytes 1048592 | tf_op jit(solution)/shard_map/psum | solution.py:13
  662.5 1.6 select_bitcast_fusion.1
  664.3 65.0 %all-reduce.13.cloned.1.call-done = (f32[2048,128]{1,0:T(8,128)}, f32[2048,128]{1,0:T(8,128)}, f32[256,128]{0,1:T(8,128)}, f32[256,128]{0,1:T(8,128)}) async-done(((f32[2048,128]{1,0:T(8,128)}, f32[2048,128]{1,0:T(8,128)}, f32[256,128]{0,1:T(8,128)}, f32[256,128]{0,1:T(8,128)}), (f32[2048,128]{1,0:T(8,128)}, f32[2048,128]{1,0:T(8,128)}, f32[256,128]{0,1:T(8,128)}, ...) | async-done | bytes 2359312 | tf_op jit(solution)/shard_map/psum | solution.py:13
  729.3 0.9 constant_dynamic-update-slice_fusion.1
  730.2 0.9 constant_dynamic-update-slice_fusion
  731.3 11.7 %cholesky.164 = f32[128,128]{1,0:T(8,128)S(1)} custom-call(f32[128,128]{1,0:T(8,128)S(1)} %cholesky.197), custom_call_target="Cholesky" | custom-call | tf_op jit(solution)/shard_map/jit(cholesky)/cholesky | solution.py:27
  743.1 9.8 %custom-call.15 = f32[1,128,128]{1,2,0:T(8,128)S(1)} custom-call(f32[1,128,128]{2,1,0:T(8,128)S(1)} %get-tuple-element.67), custom_call_target="InvertDiagBlocksLowerTriangular" | custom-call | tf_op jit(solution)/shard_map/jit(cholesky)/cholesky | solution.py:27
  753.4 11.7 %cholesky.181 = f32[128,128]{1,0:T(8,128)S(1)} custom-call(f32[128,128]{1,0:T(8,128)S(1)} %convolution_subtract_fusion.3), custom_call_target="Cholesky" | custom-call | tf_op jit(solution)/shard_map/jit(cholesky)/cholesky | solution.py:27
  765.1 0.7 compare_reduce_fusion
  765.9 0.6 compare_reduce_fusion.1
  767.9 4.1 while.5
  767.9 0.6 fusion.98
  768.5 1.4 bitcast_dynamic-update-slice_fusion.5
  769.9 0.6 fusion.98
  770.5 1.4 bitcast_dynamic-update-slice_fusion.5
  771.9 19.9 %custom-call.16 = f32[2,128,128]{1,2,0:T(8,128)S(1)} custom-call(f32[2,128,128]{2,1,0:T(8,128)S(1)} %get-tuple-element.19), custom_call_target="InvertDiagBlocksLowerTriangular" | custom-call | tf_op jit(solution)/shard_map/jit(_solve_triangular)/triangular_solve | solution.py:29
  792.8 4.7 fusion.18
  797.5 1.9 copy.90
  799.4 6.7 gather_fusion
  806.1 9.4 %copy.91 = f32[8,128,2048]{1,0,2:T(8,128)} copy(f32[8,128,2048]{2,1,0:T(8,128)} %bitcast.165) | data formatting | bytes 16777216 | tf_op jit(solution)/shard_map/jit(_take)/gather | solution.py:174
  815.5 1.0 fusion.26
  816.6 9.4 %fusion.78 = f32[2048,1024]{0,1:T(8,128)} fusion(f32[2048,256]{1,0:T(8,128)S(1)} %copy-done.2, f32[256,1024]{1,0:T(8,128)S(1)} %fusion.26), kind=kOutput, calls=%fused_computation.176 | convolution fusion | flops 6442450944 | bytes 11534336 | tf_op jit(solution)/shard_map/dot_general | solution.py:17
  825.9 9.3 %copy.94 = f32[2048,8,1,128]{3,1,0,2:T(8,128)} copy(f32[2048,8,1,128]{0,3,1,2:T(8,128)} %bitcast.164) | data formatting | bytes 16777216 | tf_op jit(solution)/shard_map/reshape | solution.py:168
  835.2 17.3 %fusion = f32[2048,8,1,128]{3,1,0,2:T(8,128)} fusion(f32[2048,8,1,128]{3,1,0,2:T(8,128)} %copy.94, f32[8,128,2048]{1,0,2:T(8,128)} %copy.91, f32[2048,8,1,128]{3,1,0,2:T(8,128)} %bitcast.167, f32[16,128,8,128]{3,2,1,0:T(8,128)} %copy-done, pred[2048]{0:T(1024)(128)(4,1)S(1)} %add_compare_fusion, pred[8,128]{1,0:T(8,128)(4,1)S(1)} %get-tuple-element.75, ...), kind=kLoop, calls=%fused_computation.6 | loop fusion | flops 10485760 | bytes 41947136 | tf_op jit(solution)/shard_map/jit(_where)/select_n | solution.py:176
  (87 shorter events, 5.0 us)
Async XLA Ops:
  7.2 7.8 copy-start.7
  7.2 62.4 %all-reduce.9.cloned.1.call-start = ((), (), s32[]{:S(2)}) async-start(), calls=%async_computation.3 | async-start | bytes 2097152 | tf_op jit(solution)/shard_map/psum | solution.py:13
  14.9 96.4 %all-reduce.15.cloned.1.call-start = ((), (), s32[]{:S(2)}) async-start(), calls=%async_computation.6 | async-start | bytes 2621440 | tf_op jit(solution)/shard_map/psum | solution.py:13
  69.6 107.8 %copy-start.5 = (f32[256,1024]{0,1:T(8,128)S(1)}, f32[256,1024]{0,1:T(8,128)}, u32[]{:S(2)}) copy-start(f32[256,1024]{0,1:T(8,128)} %all-reduce.9.cloned.1.call-done) | copy-start | bytes 3145732
  173.1 5.4 copy-start.1
  177.4 12.0 %copy-start.4 = (f32[1024,256]{1,0:T(8,128)}, f32[1024,256]{1,0:T(8,128)S(1)}, u32[]{:S(2)}) copy-start(f32[1024,256]{1,0:T(8,128)S(1)} %fusion.28) | copy-start | bytes 3145732
  199.1 53.1 %all-to-all-start = ((f32[4,2,1024,128]{3,1,2,0:T(2,128)}), f32[4,2,1024,128]{3,1,2,0:T(2,128)}, u32[]{:S(2)}, u32[]{:S(2)}) async-start(f32[4,2,1024,128]{3,1,2,0:T(2,128)} %fusion.10), calls=%async_computation | async-start | bytes 8388608 | tf_op jit(solution)/shard_map/all_to_all | solution.py:125
  269.0 99.3 %all-to-all-start.1 = ((f32[2,1024,8,128]{3,2,1,0:T(8,128)}), f32[2,1024,8,128]{3,2,1,0:T(8,128)}, u32[]{:S(2)}, u32[]{:S(2)}) async-start(f32[2,1024,8,128]{3,2,1,0:T(8,128)} %copy.80), calls=%async_computation.1 | async-start | bytes 16777216 | tf_op jit(solution)/shard_map/all_to_all | solution.py:127
  389.4 187.9 %all-to-all-start.2 = ((f32[4,2,2,128,8,128]{5,2,1,4,3,0:T(2,128)}), f32[4,2,2,128,8,128]{5,2,1,4,3,0:T(2,128)}, u32[]{:S(2)}, u32[]{:S(2)}) async-start(f32[4,2,2,128,8,128]{5,2,1,4,3,0:T(2,128)} %copy.82), calls=%async_computation.2 | async-start | bytes 16777216 | tf_op jit(solution)/shard_map/all_to_all | solution.py:138
  395.1 267.4 %all-reduce.11.cloned.1.call-start = ((), (), s32[]{:S(2)}) async-start(), calls=%async_computation.4 | async-start | bytes 2097152 | tf_op jit(solution)/shard_map/psum | solution.py:13
  601.0 6.9 copy-start
  607.9 3.4 copy-start.3
  612.9 116.4 %all-reduce.13.cloned.1.call-start = ((), (), s32[]{:S(2)}) async-start(), calls=%async_computation.5 | async-start | bytes 4718592 | tf_op jit(solution)/shard_map/psum | solution.py:13
  806.1 9.4 %copy-start.6 = (f32[256,1024]{0,1:T(8,128)S(1)}, f32[256,1024]{0,1:T(8,128)}, u32[]{:S(2)}) copy-start(f32[256,1024]{0,1:T(8,128)} %all-reduce.11.cloned.1.call-done) | copy-start | bytes 3145732
  806.1 10.5 %copy-start.2 = (f32[2048,256]{1,0:T(8,128)S(1)}, f32[2048,256]{1,0:T(8,128)}, u32[]{:S(2)}) copy-start(f32[2048,256]{1,0:T(8,128)} %fusion.18) | copy-start | bytes 6291460
Sparse Core Ops, SparseCore 0:
  15.0 54.5 all-reduce.8
  72.8 38.4 all-reduce.14
  613.0 49.4 all-reduce.10
  666.5 62.7 all-reduce.12
where the time goes:
time: 869 us; the launch traced here: 860 us
  waiting for transfers between devices  522 us (60%)
  other arithmetic  149 us (17%)
  matrix products  85.3 us (10%)
  local copies, waits for them, and re-layouts  67.9 us (8%)
  starting transfers between devices  17.6 us (2%)
  between operations  17.4 us (2%)
    psum x4, waiting for transfers between devices, spread(): return lax.psum(kept, axis)  200 us
    all_to_all x1, waiting for transfers between devices, per_device(): lax.all_to_all(row_out, 'row', split_axis=0, concat_axis=0, tiled=True)  182 us
    all_to_all x1, waiting for transfers between devices, per_device(): lax.all_to_all(leaf_out, 'leaf', split_axis=0, concat_axis=0, tiled=True)  92 us
    another operation x13, other arithmetic, lower_inverse(): lower_factor = jnp.linalg.cholesky(corner)  68.6 us
    dot_general x4, matrix products, contract(): jnp.einsum(form, left, right, precision=lax.Precision.HIGHEST, preferred_...  57.7 us
    all_to_all x1, waiting for transfers between devices, per_device(): lax.all_to_all(column_out, 'col', split_axis=0, concat_axis=0, tiled=True)  48 us
    another operation x5, other arithmetic, lower_inverse(): return jax.scipy.linalg.solve_triangular(lower_factor, identity, lower=True)  39.7 us
    dot_general x6, matrix products, matmul(): jnp.dot(left, right, precision=lax.Precision.HIGHEST, preferred_element_t...  24.9 us
  transfers between devices with their start and end apart: 7, of which 7 were waited for; matrix products, arithmetic and copies ran while one was open for 1% of the time, Pallas kernels for 0%

commit v1 on v0

v1 whole, which is shorter than its diff:
```python
import functools

import jax
import jax.numpy as jnp
from jax import lax
from jax.experimental import pallas as pl
from jax.experimental.pallas import tpu as pltpu
from jax.sharding import PartitionSpec as P

PANEL = 256
BLOCK = 128
STEP = 64
HIGH = lax.Precision.HIGHEST
F32 = jnp.float32


def dot(left, right, dims=((1,), (0,))):
    return lax.dot_general(left, right, (dims, ((), ())), precision=HIGH, preferred_element_type=F32)


def spread(x, axis, unit):
    n = lax.axis_size(axis)
    here = lax.axis_index(axis)
    stride = n // 2
    while stride >= unit:
        pairs = [
            (i + e, i + stride + e) for i in range(0, n, 2 * stride) for e in range(unit)
        ]
        got = lax.ppermute(x, axis, pairs)
        inside = here % (2 * stride)
        x = jnp.where((inside >= stride) & (inside < stride + unit), got, x)
        stride //= 2
    return x


def swap_pairs(x):
    n = lax.axis_size("col")
    here = lax.axis_index("col")
    got = lax.ppermute(x, "col", [(i, i ^ 1) for i in range(n)])
    even = here % 2 == 0
    return jnp.where(even, x, got), jnp.where(even, got, x)


def invert_kernel(left_ref, right_ref, out_ref, work):
    work[:, 0:BLOCK] = left_ref[...]
    work[:, BLOCK:PANEL] = right_ref[...]
    rows = lax.broadcasted_iota(jnp.int32, (PANEL, PANEL), 0)
    cols = lax.broadcasted_iota(jnp.int32, (PANEL, PANEL), 1)
    work[:, PANEL:] = (rows == cols).astype(F32)
    groups = STEP // 8
    sub = lax.broadcasted_iota(jnp.int32, (8, 1), 0)
    lane8 = lax.broadcasted_iota(jnp.int32, (8, BLOCK), 1)
    sub8 = lax.broadcasted_iota(jnp.int32, (8, BLOCK), 0)
    for s in range(PANEL // STEP):
        top = s * STEP
        tile = top // BLOCK * BLOCK
        off = top - tile
        d = [work[top + 8 * g : top + 8 * g + 8, tile : tile + BLOCK] for g in range(groups)]
        w = [(lane8 == sub8 + 8 * g).astype(F32) for g in range(groups)]
        for j in range(STEP):
            g0 = j // 8
            r = j % 8
            drow = d[g0][r : r + 1, :]
            wrow = w[g0][r : r + 1, :]
            inv = 1.0 / drow[:, off + j : off + j + 1]
            drow = drow * inv
            wrow = wrow * inv
            for g in range(g0, groups):
                f = d[g][:, off + j : off + j + 1]
                if g == g0:
                    if r == 7:
                        continue
                    f = jnp.where(sub > r, f, 0.0)
                d[g] = d[g] - f * drow
                w[g] = w[g] - f * wrow
        scaled = []
        for g in range(groups):
            diag = jnp.sum(jnp.where(lane8 == sub8 + (off + 8 * g), d[g], 0.0), axis=1, keepdims=True)
            scaled.append(w[g] * lax.rsqrt(diag))
        wide = jnp.concatenate(scaled, axis=0)[:, :STEP]
        strip = dot(wide, work[top : top + STEP, :])
        work[top : top + STEP, :] = strip
        if top + STEP < PANEL:
            change = dot(strip[:, :PANEL], strip, ((0,), (0,)))
            work[top + STEP :, :] = work[top + STEP :, :] - change[top + STEP :, :]
    out_ref[...] = work[:, PANEL:]


def lower_inverse(left, right):
    return pl.pallas_call(
        invert_kernel,
        out_shape=jax.ShapeDtypeStruct((PANEL, PANEL), F32),
        scratch_shapes=[pltpu.VMEM((PANEL, 2 * PANEL), F32)],
        cost_estimate=pl.CostEstimate(flops=10**10, bytes_accessed=10**8, transcendentals=0),
        name="invert",
    )(left, right)


def schur_kernel(slots, row_ids, col_ids, a_ref, f_ref, u_ref, out_ref, strip):
    strip[...] = a_ref[...] - dot(f_ref[...], u_ref[...])
    for m in range(slots):
        start = pl.multiple_of(col_ids[m] * BLOCK, BLOCK)
        out_ref[m] = strip[:, pl.ds(start, BLOCK)]


def schur_pick(front, factor, upper, row_ids, col_ids):
    dests, slots = row_ids.shape[0], col_ids.shape[0]
    width = front.shape[1]
    return pl.pallas_call(
        functools.partial(schur_kernel, slots),
        grid_spec=pltpu.PrefetchScalarGridSpec(
            num_scalar_prefetch=2,
            grid=(dests,),
            in_specs=[
                pl.BlockSpec((BLOCK, width), lambda i, r, c: (r[i], 0)),
                pl.BlockSpec((BLOCK, PANEL), lambda i, r, c: (r[i], 0)),
                pl.BlockSpec((PANEL, width), lambda i, r, c: (0, 0)),
            ],
            out_specs=pl.BlockSpec((None, slots, BLOCK, BLOCK), lambda i, r, c: (i, 0, 0, 0)),
            scratch_shapes=[pltpu.VMEM((BLOCK, width), F32)],
        ),
        out_shape=jax.ShapeDtypeStruct((dests, slots, BLOCK, BLOCK), F32),
        cost_estimate=pl.CostEstimate(
            flops=12 * dests * BLOCK * PANEL * width,
            bytes_accessed=8 * dests * BLOCK * width,
            transcendentals=0,
        ),
        name="schur",
    )(row_ids, col_ids, front, factor, upper)


def assemble_kernel(leaves, capacity, kblocks, rfrom, rok, cfrom, cok, parent_ref, *refs):
    out_ref = refs[-1]
    p = pl.program_id(0)
    for k in range(kblocks):
        total = parent_ref[pl.ds(k, BLOCK, stride=kblocks), :]
        for s in range(leaves):
            m = cfrom[s * kblocks + k]
            for t in range(capacity):
                ok = rok[(s * capacity + t) * pl.num_programs(0) + p] * cok[s * kblocks + k]
                total = total + jnp.where(ok > 0, refs[s * capacity + t][m], 0.0)
        out_ref[:, k * BLOCK : (k + 1) * BLOCK] = total


def assemble(parent, pieces, leaves, capacity, kblocks, rfrom, rok, cfrom, cok):
    per_row = parent.shape[0] // (BLOCK * kblocks)
    slots = pieces[0].shape[1]

    def piece_spec(n):
        return pl.BlockSpec(
            (None, slots, BLOCK, BLOCK), lambda i, rf, ro, cf, co: (rf[n * per_row + i], 0, 0, 0)
        )

    return pl.pallas_call(
        functools.partial(assemble_kernel, leaves, capacity, kblocks),
        grid_spec=pltpu.PrefetchScalarGridSpec(
            num_scalar_prefetch=4,
            grid=(per_row,),
            in_specs=[pl.BlockSpec((BLOCK * kblocks, BLOCK), lambda i, *_: (i, 0))]
            + [piece_spec(n) for n in range(len(pieces))],
            out_specs=pl.BlockSpec((BLOCK, kblocks * BLOCK), lambda i, *_: (i, 0)),
        ),
        out_shape=jax.ShapeDtypeStruct((per_row * BLOCK, kblocks * BLOCK), F32),
        compiler_params=pltpu.CompilerParams(vmem_limit_bytes=40 * 2**20),
        name="assemble",
    )(rfrom, rok, cfrom, cok, parent, *pieces)


def update_kernel(kblocks, lead, place, a_ref, p0_ref, p1_ref, inv_ref, top_ref, out_ref, upper):
    p = pl.program_id(0)

    @pl.when(p == 0)
    def _():
        upper[...] = dot(inv_ref[...], top_ref[...])

    factor = dot(p0_ref[...], inv_ref[:, :BLOCK], ((1,), (1,)))
    factor = factor + dot(p1_ref[...], inv_ref[:, BLOCK:], ((1,), (1,)))
    keep = (place[0] == 0) & (p < lead)
    for k in range(kblocks):
        span = slice(k * BLOCK, (k + 1) * BLOCK)
        mine = a_ref[:, span]
        value = jnp.where(keep, mine, mine - dot(factor, upper[:, span]))
        if k == 0:
            for block in range(lead):
                piece = factor[:, block * BLOCK : (block + 1) * BLOCK]
                value = jnp.where(place[1] == block, piece, value)
        out_ref[pl.ds(k, BLOCK, stride=kblocks), :] = value


def update(assembled, panel0, panel1, inverse, top, place, kblocks):
    rows, width = assembled.shape
    return pl.pallas_call(
        functools.partial(update_kernel, kblocks, PANEL // BLOCK),
        grid_spec=pltpu.PrefetchScalarGridSpec(
            num_scalar_prefetch=1,
            grid=(rows // BLOCK,),
            in_specs=[
                pl.BlockSpec((BLOCK, width), lambda i, _: (i, 0)),
                pl.BlockSpec((BLOCK, BLOCK), lambda i, _: (i, 0)),
                pl.BlockSpec((BLOCK, BLOCK), lambda i, _: (i, 0)),
                pl.BlockSpec((PANEL, PANEL), lambda i, _: (0, 0)),
                pl.BlockSpec((PANEL, width), lambda i, _: (0, 0)),
            ],
            out_specs=pl.BlockSpec((BLOCK * kblocks, BLOCK), lambda i, _: (i, 0)),
            scratch_shapes=[pltpu.VMEM((PANEL, width), F32)],
        ),
        out_shape=jax.ShapeDtypeStruct((rows * kblocks, BLOCK), F32),
        name="update",
    )(place, assembled, panel0, panel1, inverse, top)


def ranks(targets, usable):
    count = targets.shape[-1]
    same = (targets[..., :, None] == targets[..., None, :]) & usable[..., None, :]
    before = jnp.arange(count)[None, :] < jnp.arange(count)[:, None]
    return jnp.sum(same & before, axis=-1)


def per_device(child_front, parent_front, block_map):
    front = child_front[0]
    grid_rows = lax.axis_size("row")
    grid_cols = lax.axis_size("col")
    leaves = lax.axis_size("leaf")
    row_id = lax.axis_index("row")
    col_id = lax.axis_index("col")
    leaf_id = lax.axis_index("leaf")
    blocks = front.shape[0] // BLOCK
    capacity = max(1, blocks // grid_rows)
    parent_rows, kblocks = parent_front.shape[:2]
    per_row = parent_rows // BLOCK
    period = leaves * grid_cols
    lead = PANEL // BLOCK

    corner = spread(spread(front[:PANEL, :PANEL], "row", 1), "col", 1)
    corner, panel_rows, top_rows = lax.optimization_barrier(
        (corner, front[:, :PANEL], front[:PANEL, :])
    )
    panel_rows = spread(panel_rows, "col", 1)
    top_rows = spread(top_rows, "row", 1)
    inverse = lower_inverse(corner[:, :BLOCK], corner[:, BLOCK:])

    padded = jnp.concatenate([jnp.full((leaves, lead), -1, jnp.int32), block_map], axis=1)
    maps = padded.reshape(leaves, grid_rows, blocks)
    usable = maps >= 0
    to_row = jnp.where(usable, maps // per_row, -1)
    to_col = jnp.where(usable, maps % grid_cols, -1)
    row_rank = ranks(to_row, usable)
    col_rank = ranks(to_col, usable)
    positions = jnp.arange(blocks)

    def picks(target, rank, group, count):
        target = target[leaf_id, group]
        rank = rank[leaf_id, group]
        chosen = (target == jnp.arange(count)[:, None, None]) & (
            rank == jnp.arange(capacity)[None, :, None]
        )
        return jnp.sum(jnp.where(chosen, positions, 0), axis=-1).astype(jnp.int32)

    row_ids = picks(to_row, row_rank, row_id, grid_rows)
    col_ids = picks(to_col, col_rank, col_id, grid_cols).reshape(-1)

    order = (leaf_id - jnp.arange(leaves)) % leaves
    maps_here = maps[order]
    row_rank_here = row_rank[order]
    col_rank_here = col_rank[order]
    group = jnp.arange(grid_rows)[None, None, :, None]
    hit = maps_here[:, None] == (row_id * per_row + jnp.arange(per_row))[None, :, None, None]
    in_chunk = row_rank_here[:, None, None] == jnp.arange(capacity)[None, :, None, None, None]
    hit_chunk = hit[:, None] & in_chunk
    rfrom = jnp.sum(jnp.where(hit_chunk, group[:, None], 0), axis=(-1, -2))
    rok = jnp.sum(hit_chunk, axis=(-1, -2))
    owned = jnp.arange(kblocks) * period + leaf_id * grid_cols + col_id
    hit = maps_here[:, None] == owned[None, :, None, None]
    slot = group * capacity + col_rank_here[:, None]
    cfrom = jnp.sum(jnp.where(hit, slot, 0), axis=(-1, -2))
    cok = jnp.sum(hit, axis=(-1, -2))
    rfrom, rok, cfrom, cok = [x.reshape(-1).astype(jnp.int32) for x in (rfrom, rok, cfrom, cok)]

    factor = dot(panel_rows, inverse, ((1,), (1,)))
    upper = dot(inverse, top_rows)
    own = []
    for t in range(capacity):
        out = schur_pick(front, factor, upper, row_ids[:, t], col_ids)
        out = out.reshape(grid_rows * grid_cols, capacity, BLOCK, BLOCK)
        got = lax.all_to_all(out, ("row", "col"), split_axis=0, concat_axis=0, tiled=True)
        own.append(got)
    pieces = [[] for _ in range(leaves)]
    for got in own:
        for shift in range(leaves):
            moved = got
            if shift:
                pairs = [(i, (i + shift) % leaves) for i in range(leaves)]
                moved = lax.ppermute(got, "leaf", pairs)
            pieces[shift].append(
                moved.reshape(grid_rows, grid_cols * capacity, BLOCK, BLOCK)
            )
    pieces = [x for part in pieces for x in part]
    assembled = assemble(
        parent_front.reshape(parent_rows * kblocks, BLOCK),
        pieces, leaves, capacity, kblocks, rfrom, rok, cfrom, cok,
    )

    piece = spread(spread(assembled[:PANEL, :BLOCK], "col", 2), "leaf", 1)
    piece, panel = lax.optimization_barrier((piece, assembled[:, :BLOCK]))
    panel = spread(spread(panel, "col", 2), "leaf", 1)
    panel0, panel1 = swap_pairs(panel)
    corner0, corner1 = swap_pairs(spread(piece, "row", 1))
    corner0, corner1, top = lax.optimization_barrier((corner0, corner1, assembled[:PANEL]))
    top = spread(top, "row", 1)
    inverse_parent = lower_inverse(corner0, corner1)
    place = jnp.stack([row_id, leaf_id * grid_cols + col_id]).astype(jnp.int32)
    result = update(assembled, panel0, panel1, inverse_parent, top, place, kblocks)
    return factor[None], result.reshape(parent_front.shape)


def solution(mesh):
    placed = (P("leaf", "row", "col"), P("row", None, ("leaf", "col"), None), P())
    return jax.shard_map(
        per_device,
        mesh=mesh,
        in_specs=placed,
        out_specs=(P("leaf", "row", None), P("row", None, ("leaf", "col"), None)),
        check_vma=False,
    )
```

time: 869 us -> 402 us (0.46)
  waiting for transfers between devices: 522 us -> 178 us
  other arithmetic: 149 us -> 10.3 us
  Pallas kernels: 0 us -> 112 us
  matrix products: 85.3 us -> 5.94 us
  starting transfers between devices: 17.6 us -> 76.4 us
  local copies, waits for them, and re-layouts: 67.9 us -> 12 us
  between operations: 17.4 us -> 1.03 us
    all_to_all x3 -> x2, waiting for transfers between devices: 322 us -> 74.2 us  [per_device(): lax.all_to_all(out, ('row', 'col'), split_axis=0, concat_axis=0, tiled=True)]
    psum x4 -> x0, waiting for transfers between devices: 200 us -> none  [spread(): return lax.psum(kept, axis)]
    pallas_call x0 -> x6, Pallas kernels: none -> 112 us  [the longest x2 51.1 us: lower_inverse(): pl.pallas_call(invert_kernel, out_shape=jax.ShapeDtypeStruct((PANEL, PANE...]
    another operation x18 -> x1, other arithmetic: 108 us -> 0.65 us  [per_device(): place = jnp.stack([row_id, leaf_id * grid_cols + col_id]).astype(jnp.int32)]
    ppermute x0 -> x20, waiting for transfers between devices: none -> 103 us  [the longest x16 55.6 us: spread(): got = lax.ppermute(x, axis, pairs)]
    dot_general x10 -> x2, matrix products: 82.6 us -> 5.94 us  [dot(): lax.dot_general(left, right, (dims, ((), ())), precision=HIGH, preferred_...]
    ppermute x0 -> x20, starting transfers between devices: none -> 60.3 us  [the longest x16 57.1 us: spread(): got = lax.ppermute(x, axis, pairs)]
    select_n x9 -> x18, other arithmetic: 26.5 us -> 8.39 us  [the longest x14 6.19 us: spread(): x = jnp.where((inside >= stride) & (inside < stride + unit), got, x)]
  transfers between devices with their start and end apart: 7 -> 22, of which waited for: 7 -> 15; matrix products, arithmetic and copies ran while one was open for 1% -> 5% of each run, Pallas kernels for 0% -> 15%
where the time goes in v1:
time: 402 us; the launch traced here: 396 us
  waiting for transfers between devices  178 us (44%)
  Pallas kernels  112 us (28%)
  starting transfers between devices  76.4 us (19%)
  local copies, waits for them, and re-layouts  12 us (3%)
  other arithmetic  10.3 us (3%)
  matrix products  5.94 us (1%)
    all_to_all x2, waiting for transfers between devices, per_device(): lax.all_to_all(out, ('row', 'col'), split_axis=0, concat_axis=0, tiled=True)  74.2 us
    ppermute x16, starting transfers between devices, spread(): got = lax.ppermute(x, axis, pairs)  57.1 us
    ppermute x16, waiting for transfers between devices, spread(): got = lax.ppermute(x, axis, pairs)  55.6 us
    pallas_call x2, Pallas kernels, lower_inverse(): pl.pallas_call(invert_kernel, out_shape=jax.ShapeDtypeStruct((PANEL, PANE...  51.1 us
    ppermute x2, waiting for transfers between devices, per_device(): moved = lax.ppermute(got, 'leaf', pairs)  47.7 us
    pallas_call x1, Pallas kernels, update(): pl.pallas_call(functools.partial(update_kernel, kblocks, PANEL // BLOCK),...  32.2 us
    pallas_call x1, Pallas kernels, assemble(): pl.pallas_call(functools.partial(assemble_kernel, leaves, capacity, kbloc...  16.2 us
    all_to_all x2, starting transfers between devices, per_device(): lax.all_to_all(out, ('row', 'col'), split_axis=0, concat_axis=0, tiled=True)  16 us
  transfers between devices with their start and end apart: 22, of which 15 were waited for; matrix products, arithmetic and copies ran while one was open for 5% of the time, Pallas kernels for 15%

profile of v1, /device:TPU:0, one launch (start us, length us, event | category | flops | bytes accessed | tf_op | source)
XLA Modules:
  0.0 395.6 jit_solution(990392609854524649)
XLA Ops:
  0.6 1.0 slice.50
  1.6 6.0 %collective-permute-start = (f32[256,256]{1,0:T(8,128)S(1)}, f32[256,256]{1,0:T(8,128)S(1)}, u32[]{:S(2)}, u32[]{:S(2)}) collective-permute-start(f32[256,256]{1,0:T(8,128)S(1)} %slice.50), channel_id=1, source_target_pairs={{0,8},{1,9},{2,10},{3,11},{16,24},{17,25},{18,26},{19,27}} | collective-permute-start | bytes 786440 | tf_op jit(solution)/shard_map/ppermute | solution.py:29
  7.6 0.8 concatenate.3
  8.5 0.4 convert_reduce_fusion
  8.9 4.2 %collective-permute-done = f32[256,256]{1,0:T(8,128)S(1)} collective-permute-done((f32[256,256]{1,0:T(8,128)S(1)}, f32[256,256]{1,0:T(8,128)S(1)}, u32[]{:S(2)}, u32[]{:S(2)}) %collective-permute-start) | collective-permute-done | bytes 262176 | tf_op jit(solution)/shard_map/ppermute | solution.py:29
  13.1 1.0 broadcast_select_fusion.8
  14.1 1.3 collective-permute-start.1
  15.4 4.9 %collective-permute-done.1 = f32[256,256]{1,0:T(8,128)S(1)} collective-permute-done((f32[256,256]{1,0:T(8,128)S(1)}, f32[256,256]{1,0:T(8,128)S(1)}, u32[]{:S(2)}, u32[]{:S(2)}) %collective-permute-start.1) | collective-permute-done | bytes 262176 | tf_op jit(solution)/shard_map/ppermute | solution.py:29
  20.4 3.4 collective-permute-start.2
  23.8 1.3 slice.51
  25.2 2.4 collective-permute-done.2
  27.7 1.3 collective-permute-start.3
  29.0 1.3 slice_bitcast_fusion
  30.4 5.4 %collective-permute-start.4 = (f32[1024,256]{1,0:T(8,128)S(1)}, f32[1024,256]{1,0:T(8,128)}, u32[]{:S(2)}, u32[]{:S(2)}) collective-permute-start(f32[1024,256]{1,0:T(8,128)S(1)} %slice.51), channel_id=1, source_target_pairs={{0,2},{4,6},{8,10},{12,14},{16,18},{20,22},{24,26},{28,30}} | collective-permute-start | bytes 3145736 | tf_op jit(solution)/shard_map/ppermute | solution.py:29
  36.0 0.6 reshape.362.col_ids
  36.6 5.3 %collective-permute-start.6 = (f32[256,1024]{1,0:T(8,128)S(1)}, f32[256,1024]{1,0:T(8,128)S(1)}, u32[]{:S(2)}, u32[]{:S(2)}) collective-permute-start(f32[256,1024]{1,0:T(8,128)S(1)} %slice_bitcast_fusion), channel_id=1, source_target_pairs={{0,8},{1,9},{2,10},{3,11},{16,24},{17,25},{18,26},{19,27}} | collective-permute-start | bytes 3145736 | tf_op jit(solution)/shard_map/ppermute | solution.py:29
  42.1 0.6 slice_bitcast_fusion.1
  42.7 0.7 fusion.20
  43.4 3.7 collective-permute-done.4
  47.2 2.3 collective-permute-start.5
  49.5 13.9 %collective-permute-done.6 = f32[256,1024]{1,0:T(8,128)S(1)} collective-permute-done((f32[256,1024]{1,0:T(8,128)S(1)}, f32[256,1024]{1,0:T(8,128)S(1)}, u32[]{:S(2)}, u32[]{:S(2)}) %collective-permute-start.6) | collective-permute-done | bytes 1048608 | tf_op jit(solution)/shard_map/ppermute | solution.py:29
  63.6 1.4 collective-permute-start.7
  65.0 25.5 %invert.2 = f32[256,256]{1,0:T(8,128)} custom-call(f32[256,128]{1,0:T(8,128)} %get-tuple-element.35.left_ref, f32[256,128]{1,0:T(8,128)} %get-tuple-element.34.right_ref), custom_call_target="tpu_custom_call" | custom-call | flops 10000000000 | bytes 100000000 | tf_op jit(solution)/shard_map/invert/pallas_call | solution.py:90
  90.5 2.9 fusion.2.f_ref
  93.5 3.0 fusion.u_ref
  96.5 6.4 %schur.2 = f32[4,8,128,128]{3,2,1,0:T(8,128)} custom-call(s32[4]{0:T(128)} %get-tuple-element.39.row_ids, s32[8]{0:T(128)} %reshape.362.col_ids, f32[1024,1024]{1,0:T(8,128)} %bitcast.36, f32[1024,256]{1,0:T(8,128)} %fusion.2.f_ref, f32[256,1024]{1,0:T(8,128)} %fusion.u_ref), custom_call_target="tpu_custom_call" | custom-call | flops 1610612736 | bytes 4194304 | tf_op jit(solution)/shard_map/schur/pallas_call | solution.py:109
  102.9 4.8 %all-to-all-start = ((f32[16,2,128,128]{3,2,1,0:T(8,128)}), f32[16,2,128,128]{3,2,1,0:T(8,128)S(1)}, u32[]{:S(2)}, u32[]{:S(2)}) async-start(f32[16,2,128,128]{3,2,1,0:T(8,128)} %bitcast.41), calls=%async_computation | async-start | bytes 4194304 | tf_op jit(solution)/shard_map/all_to_all | solution.py:285
  107.7 6.4 %schur.3 = f32[4,8,128,128]{3,2,1,0:T(8,128)} custom-call(s32[4]{0:T(128)} %get-tuple-element.38.row_ids, s32[8]{0:T(128)} %reshape.362.col_ids, f32[1024,1024]{1,0:T(8,128)} %bitcast.37, f32[1024,256]{1,0:T(8,128)} %fusion.2.f_ref, f32[256,1024]{1,0:T(8,128)} %fusion.u_ref), custom_call_target="tpu_custom_call" | custom-call | flops 1610612736 | bytes 4194304 | tf_op jit(solution)/shard_map/schur/pallas_call | solution.py:109
  114.1 34.7 %all-to-all-done = f32[16,2,128,128]{3,2,1,0:T(8,128)S(1)} async-done(((f32[16,2,128,128]{3,2,1,0:T(8,128)}), f32[16,2,128,128]{3,2,1,0:T(8,128)S(1)}, u32[]{:S(2)}, u32[]{:S(2)}) %all-to-all-start) | async-done | bytes 2097184 | tf_op jit(solution)/shard_map/all_to_all | solution.py:285
  148.8 11.3 %all-to-all-start.1 = ((f32[16,2,128,128]{3,2,1,0:T(8,128)}), f32[16,2,128,128]{3,2,1,0:T(8,128)}, u32[]{:S(2)}, u32[]{:S(2)}) async-start(f32[16,2,128,128]{3,2,1,0:T(8,128)} %bitcast.40), calls=%async_computation.1 | async-start | bytes 4194304 | tf_op jit(solution)/shard_map/all_to_all | solution.py:285
  160.0 1.6 collective-permute-start.8
  161.6 39.6 %all-to-all-done.1 = f32[16,2,128,128]{3,2,1,0:T(8,128)} async-done(((f32[16,2,128,128]{3,2,1,0:T(8,128)}), f32[16,2,128,128]{3,2,1,0:T(8,128)}, u32[]{:S(2)}, u32[]{:S(2)}) %all-to-all-start.1) | async-done | bytes 2097184 | tf_op jit(solution)/shard_map/all_to_all | solution.py:285
  201.2 1.5 collective-permute-start.9
  202.7 0.6 gather_fusion
  203.3 0.6 gather_fusion.2
  203.9 0.6 gather_fusion.1
  205.3 3.4 collective-permute-done.8
  208.7 44.3 %collective-permute-done.9 = f32[16,2,128,128]{3,2,1,0:T(8,128)} collective-permute-done((f32[16,2,128,128]{3,2,1,0:T(8,128)}, f32[16,2,128,128]{3,2,1,0:T(8,128)}, u32[]{:S(2)}, u32[]{:S(2)}) %collective-permute-start.9) | collective-permute-done | bytes 2097184 | tf_op jit(solution)/shard_map/ppermute | solution.py:293
  253.0 16.2 %assemble.1.a_ref = f32[2048,1024]{1,0:T(8,128)} custom-call(s32[64]{0:T(128)S(1)} %reshape.357.rfrom, s32[64]{0:T(128)S(1)} %reshape.358.rok, s32[16]{0:T(128)S(1)} %reshape.359.cfrom, s32[16]{0:T(128)S(1)} %reshape.360.cok, f32[16384,128]{1,0:T(8,128)} %bitcast.39, f32[4,8,128,128]{3,2,1,0:T(8,128)S(1)} %bitcast.32, f32[4,8,128,128]{3,2,1,0:T(8,128)} %bitcast.16.refs_1_, ...), custom_call_target="tpu_custom_call" | custom-call | tf_op jit(solution)/shard_map/assemble/pallas_call | solution.py:154
  269.2 0.9 slice.52
  270.1 3.6 collective-permute-start.10
  273.7 2.5 collective-permute-done.10
  276.2 0.9 broadcast_select_fusion.16
  277.1 3.4 collective-permute-start.11
  280.6 1.3 slice.53
  281.9 1.2 collective-permute-done.11
  283.1 5.2 %collective-permute-start.15 = (f32[256,128]{1,0:T(8,128)S(1)}, f32[256,128]{1,0:T(8,128)S(1)}, u32[]{:S(2)}, u32[]{:S(2)}) collective-permute-start(f32[256,128]{1,0:T(8,128)S(1)} %broadcast_select_fusion.17), channel_id=1, source_target_pairs={{0,8},{1,9},{2,10},{3,11},{16,24},{17,25},{18,26},{19,27}} | collective-permute-start | bytes 393224 | tf_op jit(solution)/shard_map/ppermute | solution.py:29
  288.3 5.4 %collective-permute-start.12 = (f32[2048,128]{1,0:T(8,128)S(1)}, f32[2048,128]{1,0:T(8,128)}, u32[]{:S(2)}, u32[]{:S(2)}) collective-permute-start(f32[2048,128]{1,0:T(8,128)S(1)} %slice.53), channel_id=1, source_target_pairs={{0,2},{1,3},{4,6},{5,7},{8,10},{9,11},{12,14},{13,15},{16,18},{17,... | collective-permute-start | bytes 3145736 | tf_op jit(solution)/shard_map/ppermute | solution.py:29
  293.7 1.8 collective-permute-start.16
  295.5 2.5 collective-permute-done.16
  298.1 1.3 slice.54
  299.4 0.7 broadcast_select_fusion.14
  300.2 4.0 %collective-permute-start.18 = (f32[256,1024]{1,0:T(8,128)S(1)}, f32[256,1024]{1,0:T(8,128)}, u32[]{:S(2)}, u32[]{:S(2)}) collective-permute-start(f32[256,1024]{1,0:T(8,128)S(1)} %slice.54), channel_id=1, source_target_pairs={{0,8},{1,9},{2,10},{3,11},{16,24},{17,25},{18,26},{19,27}} | collective-permute-start | bytes 3145736 | tf_op jit(solution)/shard_map/ppermute | solution.py:29
  304.1 7.5 %collective-permute-done.12 = f32[2048,128]{1,0:T(8,128)} collective-permute-done((f32[2048,128]{1,0:T(8,128)S(1)}, f32[2048,128]{1,0:T(8,128)}, u32[]{:S(2)}, u32[]{:S(2)}) %collective-permute-start.12) | collective-permute-done | bytes 1048608 | tf_op jit(solution)/shard_map/ppermute | solution.py:29
  311.8 5.1 %collective-permute-start.13 = (f32[2048,128]{1,0:T(8,128)S(1)}, f32[2048,128]{1,0:T(8,128)}, u32[]{:S(2)}, u32[]{:S(2)}) collective-permute-start(f32[2048,128]{1,0:T(8,128)S(1)} %broadcast_select_fusion), channel_id=1, source_target_pairs={{0,16},{1,17},{2,18},{3,19},{4,20},{5,21},{6,22},{7,23},{8,24},{9,... | collective-permute-start | bytes 3145736 | tf_op jit(solution)/shard_map/ppermute | solution.py:29
  316.9 0.7 pad_add_fusion.place
  317.6 8.7 %collective-permute-done.18 = f32[256,1024]{1,0:T(8,128)} collective-permute-done((f32[256,1024]{1,0:T(8,128)S(1)}, f32[256,1024]{1,0:T(8,128)}, u32[]{:S(2)}, u32[]{:S(2)}) %collective-permute-start.18) | collective-permute-done | bytes 1048608 | tf_op jit(solution)/shard_map/ppermute | solution.py:29
  326.2 1.1 broadcast_select_fusion.4
  327.3 2.2 collective-permute-start.19
  329.6 4.1 %collective-permute-done.13 = f32[2048,128]{1,0:T(8,128)} collective-permute-done((f32[2048,128]{1,0:T(8,128)S(1)}, f32[2048,128]{1,0:T(8,128)}, u32[]{:S(2)}, u32[]{:S(2)}) %collective-permute-start.13) | collective-permute-done | bytes 1048608 | tf_op jit(solution)/shard_map/ppermute | solution.py:29
  333.9 25.6 %invert.3.inv_ref = f32[256,256]{1,0:T(8,128)} custom-call(f32[256,128]{1,0:T(8,128)} %get-tuple-element.15.left_ref, f32[256,128]{1,0:T(8,128)} %get-tuple-element.16.right_ref), custom_call_target="tpu_custom_call" | custom-call | flops 10000000000 | bytes 100000000 | tf_op jit(solution)/shard_map/invert/pallas_call | solution.py:90
  359.4 2.5 broadcast_select_fusion.6.top_ref
  361.9 1.4 broadcast_select_fusion.2
  363.4 32.2 %update.1 = f32[16384,128]{1,0:T(8,128)} custom-call(s32[2]{0:T(128)} %pad_add_fusion.place, f32[2048,1024]{1,0:T(8,128)} %assemble.1.a_ref, f32[2048,128]{1,0:T(8,128)} %get-tuple-element.31.p0_ref, f32[2048,128]{1,0:T(8,128)} %get-tuple-element.30.p1_ref, f32[256,256]{1,0:T(8,128)} %invert.3.inv_ref, f32[256,1024]{1,0:T(8,128)} %broadcast_select_fusion.6.top_ref), custom_call_target="tpu_custom_call" | custom-call | tf_op jit(solution)/shard_map/update/pallas_call | solution.py:192
  (46 shorter events, 2.3 us)
Async XLA Ops:
  1.6 11.5 %collective-permute-start = (f32[256,256]{1,0:T(8,128)S(1)}, f32[256,256]{1,0:T(8,128)S(1)}, u32[]{:S(2)}, u32[]{:S(2)}) collective-permute-start(f32[256,256]{1,0:T(8,128)S(1)} %slice.50), channel_id=1, source_target_pairs={{0,8},{1,9},{2,10},{3,11},{16,24},{17,25},{18,26},{19,27}} | collective-permute-start | bytes 786440 | tf_op jit(solution)/shard_map/ppermute | solution.py:29
  14.1 6.3 %collective-permute-start.1 = (f32[256,256]{1,0:T(8,128)S(1)}, f32[256,256]{1,0:T(8,128)S(1)}, u32[]{:S(2)}, u32[]{:S(2)}) collective-permute-start(f32[256,256]{1,0:T(8,128)S(1)} %broadcast_select_fusion.8), channel_id=1, source_target_pairs={{0,4},{8,12},{1,5},{9,13},{2,6},{10,14},{3,7},{11,15},{16,20},{24,... | collective-permute-start | bytes 786440 | tf_op jit(solution)/shard_map/ppermute | solution.py:29
  20.4 7.3 %collective-permute-start.2 = (f32[256,256]{1,0:T(8,128)S(1)}, f32[256,256]{1,0:T(8,128)S(1)}, u32[]{:S(2)}, u32[]{:S(2)}) collective-permute-start(f32[256,256]{1,0:T(8,128)S(1)} %broadcast_select_fusion.9), channel_id=1, source_target_pairs={{0,2},{4,6},{8,10},{12,14},{16,18},{20,22},{24,26},{28,30}} | collective-permute-start | bytes 786440 | tf_op jit(solution)/shard_map/ppermute | solution.py:29
  27.7 2.6 collective-permute-start.3
  30.4 16.7 %collective-permute-start.4 = (f32[1024,256]{1,0:T(8,128)S(1)}, f32[1024,256]{1,0:T(8,128)}, u32[]{:S(2)}, u32[]{:S(2)}) collective-permute-start(f32[1024,256]{1,0:T(8,128)S(1)} %slice.51), channel_id=1, source_target_pairs={{0,2},{4,6},{8,10},{12,14},{16,18},{20,22},{24,26},{28,30}} | collective-permute-start | bytes 3145736 | tf_op jit(solution)/shard_map/ppermute | solution.py:29
  36.6 26.8 %collective-permute-start.6 = (f32[256,1024]{1,0:T(8,128)S(1)}, f32[256,1024]{1,0:T(8,128)S(1)}, u32[]{:S(2)}, u32[]{:S(2)}) collective-permute-start(f32[256,1024]{1,0:T(8,128)S(1)} %slice_bitcast_fusion), channel_id=1, source_target_pairs={{0,8},{1,9},{2,10},{3,11},{16,24},{17,25},{18,26},{19,27}} | collective-permute-start | bytes 3145736 | tf_op jit(solution)/shard_map/ppermute | solution.py:29
  47.2 43.3 %collective-permute-start.5 = (f32[1024,256]{1,0:T(8,128)S(1)}, f32[1024,256]{1,0:T(8,128)}, u32[]{:S(2)}, u32[]{:S(2)}) collective-permute-start(f32[1024,256]{1,0:T(8,128)S(1)} %broadcast_select_fusion.7), channel_id=1, source_target_pairs={{0,1},{2,3},{4,5},{6,7},{8,9},{10,11},{12,13},{14,15},{16,17},{18,... | collective-permute-start | bytes 3145736 | tf_op jit(solution)/shard_map/ppermute | solution.py:29
  63.6 29.9 %collective-permute-start.7 = (f32[256,1024]{1,0:T(8,128)S(1)}, f32[256,1024]{1,0:T(8,128)S(1)}, u32[]{:S(2)}, u32[]{:S(2)}) collective-permute-start(f32[256,1024]{1,0:T(8,128)S(1)} %broadcast_select_fusion.5), channel_id=1, source_target_pairs={{0,4},{8,12},{1,5},{9,13},{2,6},{10,14},{3,7},{11,15},{16,20},{24,... | collective-permute-start | bytes 3145736 | tf_op jit(solution)/shard_map/ppermute | solution.py:29
  102.9 45.9 %all-to-all-start = ((f32[16,2,128,128]{3,2,1,0:T(8,128)}), f32[16,2,128,128]{3,2,1,0:T(8,128)S(1)}, u32[]{:S(2)}, u32[]{:S(2)}) async-start(f32[16,2,128,128]{3,2,1,0:T(8,128)} %bitcast.41), calls=%async_computation | async-start | bytes 4194304 | tf_op jit(solution)/shard_map/all_to_all | solution.py:285
  148.8 52.4 %all-to-all-start.1 = ((f32[16,2,128,128]{3,2,1,0:T(8,128)}), f32[16,2,128,128]{3,2,1,0:T(8,128)}, u32[]{:S(2)}, u32[]{:S(2)}) async-start(f32[16,2,128,128]{3,2,1,0:T(8,128)} %bitcast.40), calls=%async_computation.1 | async-start | bytes 4194304 | tf_op jit(solution)/shard_map/all_to_all | solution.py:285
  160.0 48.6 %collective-permute-start.8 = (f32[16,2,128,128]{3,2,1,0:T(8,128)S(1)}, f32[16,2,128,128]{3,2,1,0:T(8,128)}, u32[]{:S(2)}, u32[]{:S(2)}) collective-permute-start(f32[16,2,128,128]{3,2,1,0:T(8,128)S(1)} %all-to-all-done), channel_id=1, source_target_pairs={{0,16},{16,0},{1,17},{17,1},{2,18},{18,2},{3,19},{19,3},{4,20},{20... | collective-permute-start | bytes 6291464 | tf_op jit(solution)/shard_map/ppermute | solution.py:293
  201.2 51.8 %collective-permute-start.9 = (f32[16,2,128,128]{3,2,1,0:T(8,128)}, f32[16,2,128,128]{3,2,1,0:T(8,128)}, u32[]{:S(2)}, u32[]{:S(2)}) collective-permute-start(f32[16,2,128,128]{3,2,1,0:T(8,128)} %all-to-all-done.1), channel_id=1, source_target_pairs={{0,16},{16,0},{1,17},{17,1},{2,18},{18,2},{3,19},{19,3},{4,20},{20... | collective-permute-start | bytes 6291464 | tf_op jit(solution)/shard_map/ppermute | solution.py:293
  270.1 6.1 %collective-permute-start.10 = (f32[256,128]{1,0:T(8,128)S(1)}, f32[256,128]{1,0:T(8,128)S(1)}, u32[]{:S(2)}, u32[]{:S(2)}) collective-permute-start(f32[256,128]{1,0:T(8,128)S(1)} %slice.52), channel_id=1, source_target_pairs={{0,2},{1,3},{4,6},{5,7},{8,10},{9,11},{12,14},{13,15},{16,18},{17,... | collective-permute-start | bytes 393224 | tf_op jit(solution)/shard_map/ppermute | solution.py:29
  277.1 5.9 %collective-permute-start.11 = (f32[256,128]{1,0:T(8,128)S(1)}, f32[256,128]{1,0:T(8,128)S(1)}, u32[]{:S(2)}, u32[]{:S(2)}) collective-permute-start(f32[256,128]{1,0:T(8,128)S(1)} %broadcast_select_fusion.16), channel_id=1, source_target_pairs={{0,16},{1,17},{2,18},{3,19},{4,20},{5,21},{6,22},{7,23},{8,24},{9,... | collective-permute-start | bytes 393224 | tf_op jit(solution)/shard_map/ppermute | solution.py:29
  283.1 10.7 %collective-permute-start.15 = (f32[256,128]{1,0:T(8,128)S(1)}, f32[256,128]{1,0:T(8,128)S(1)}, u32[]{:S(2)}, u32[]{:S(2)}) collective-permute-start(f32[256,128]{1,0:T(8,128)S(1)} %broadcast_select_fusion.17), channel_id=1, source_target_pairs={{0,8},{1,9},{2,10},{3,11},{16,24},{17,25},{18,26},{19,27}} | collective-permute-start | bytes 393224 | tf_op jit(solution)/shard_map/ppermute | solution.py:29
  288.3 23.4 %collective-permute-start.12 = (f32[2048,128]{1,0:T(8,128)S(1)}, f32[2048,128]{1,0:T(8,128)}, u32[]{:S(2)}, u32[]{:S(2)}) collective-permute-start(f32[2048,128]{1,0:T(8,128)S(1)} %slice.53), channel_id=1, source_target_pairs={{0,2},{1,3},{4,6},{5,7},{8,10},{9,11},{12,14},{13,15},{16,18},{17,... | collective-permute-start | bytes 3145736 | tf_op jit(solution)/shard_map/ppermute | solution.py:29
  293.7 4.3 %collective-permute-start.16 = (f32[256,128]{1,0:T(8,128)S(1)}, f32[256,128]{1,0:T(8,128)S(1)}, u32[]{:S(2)}, u32[]{:S(2)}) collective-permute-start(f32[256,128]{1,0:T(8,128)S(1)} %broadcast_select_fusion.12), channel_id=1, source_target_pairs={{0,4},{8,12},{1,5},{9,13},{2,6},{10,14},{3,7},{11,15},{16,20},{24,... | collective-permute-start | bytes 393224 | tf_op jit(solution)/shard_map/ppermute | solution.py:29
  298.0 1.4 collective-permute-start.17
  300.2 26.1 %collective-permute-start.18 = (f32[256,1024]{1,0:T(8,128)S(1)}, f32[256,1024]{1,0:T(8,128)}, u32[]{:S(2)}, u32[]{:S(2)}) collective-permute-start(f32[256,1024]{1,0:T(8,128)S(1)} %slice.54), channel_id=1, source_target_pairs={{0,8},{1,9},{2,10},{3,11},{16,24},{17,25},{18,26},{19,27}} | collective-permute-start | bytes 3145736 | tf_op jit(solution)/shard_map/ppermute | solution.py:29
  311.8 21.9 %collective-permute-start.13 = (f32[2048,128]{1,0:T(8,128)S(1)}, f32[2048,128]{1,0:T(8,128)}, u32[]{:S(2)}, u32[]{:S(2)}) collective-permute-start(f32[2048,128]{1,0:T(8,128)S(1)} %broadcast_select_fusion), channel_id=1, source_target_pairs={{0,16},{1,17},{2,18},{3,19},{4,20},{5,21},{6,22},{7,23},{8,24},{9,... | collective-permute-start | bytes 3145736 | tf_op jit(solution)/shard_map/ppermute | solution.py:29
  327.3 32.1 %collective-permute-start.19 = (f32[256,1024]{1,0:T(8,128)}, f32[256,1024]{1,0:T(8,128)}, u32[]{:S(2)}, u32[]{:S(2)}) collective-permute-start(f32[256,1024]{1,0:T(8,128)} %broadcast_select_fusion.4), channel_id=1, source_target_pairs={{0,4},{8,12},{1,5},{9,13},{2,6},{10,14},{3,7},{11,15},{16,20},{24,... | collective-permute-start | bytes 3145736 | tf_op jit(solution)/shard_map/ppermute | solution.py:29
  333.8 28.1 %collective-permute-start.14 = (f32[2048,128]{1,0:T(8,128)S(1)}, f32[2048,128]{1,0:T(8,128)S(1)}, u32[]{:S(2)}, u32[]{:S(2)}) collective-permute-start(f32[2048,128]{1,0:T(8,128)S(1)} %broadcast_select_fusion.1), channel_id=1, source_target_pairs={{0,1},{1,0},{2,3},{3,2},{4,5},{5,4},{6,7},{7,6},{8,9},{9,8},{10,11... | collective-permute-start | bytes 3145736 | tf_op jit(solution)/shard_map/ppermute | solution.py:39

commit v2 on v1

v2 whole, which is shorter than its diff:
```python
import functools

import jax
import jax.numpy as jnp
from jax import lax
from jax.experimental import pallas as pl
from jax.experimental.pallas import tpu as pltpu
from jax.sharding import PartitionSpec as P

PANEL = 256
BLOCK = 128
STEP = 64
HIGH = lax.Precision.HIGHEST
F32 = jnp.float32


def dot(left, right, dims=((1,), (0,))):
    return lax.dot_general(left, right, (dims, ((), ())), precision=HIGH, preferred_element_type=F32)


def split(x):
    high = x.astype(jnp.bfloat16)
    return high, (x - high.astype(F32)).astype(jnp.bfloat16)


def dot_split(left, right):
    one = lambda a, b: jnp.dot(a, b, preferred_element_type=F32)
    return one(left[0], right[0]) + (one(left[0], right[1]) + one(left[1], right[0]))


def spread(x, axis, unit):
    n = lax.axis_size(axis)
    here = lax.axis_index(axis)
    stride = n // 2
    while stride >= unit:
        pairs = [
            (i + e, i + stride + e) for i in range(0, n, 2 * stride) for e in range(unit)
        ]
        got = lax.ppermute(x, axis, pairs)
        inside = here % (2 * stride)
        x = jnp.where((inside >= stride) & (inside < stride + unit), got, x)
        stride //= 2
    return x


def swap_pairs(x):
    n = lax.axis_size("col")
    here = lax.axis_index("col")
    got = lax.ppermute(x, "col", [(i, i ^ 1) for i in range(n)])
    even = here % 2 == 0
    return jnp.where(even, x, got), jnp.where(even, got, x)


def invert_kernel(left_ref, right_ref, out_ref, work):
    work[:, 0:BLOCK] = left_ref[...]
    work[:, BLOCK:PANEL] = right_ref[...]
    rows = lax.broadcasted_iota(jnp.int32, (PANEL, PANEL), 0)
    cols = lax.broadcasted_iota(jnp.int32, (PANEL, PANEL), 1)
    work[:, PANEL:] = (rows == cols).astype(F32)
    groups = STEP // 8
    sub = lax.broadcasted_iota(jnp.int32, (8, 1), 0)
    lane8 = lax.broadcasted_iota(jnp.int32, (8, BLOCK), 1)
    sub8 = lax.broadcasted_iota(jnp.int32, (8, BLOCK), 0)
    for s in range(PANEL // STEP):
        top = s * STEP
        tile = top // BLOCK * BLOCK
        off = top - tile
        d = [work[top + 8 * g : top + 8 * g + 8, tile : tile + BLOCK] for g in range(groups)]
        w = [(lane8 == sub8 + 8 * g).astype(F32) for g in range(groups)]
        for j in range(STEP):
            g0 = j // 8
            r = j % 8
            drow = d[g0][r : r + 1, :]
            wrow = w[g0][r : r + 1, :]
            inv = 1.0 / drow[:, off + j : off + j + 1]
            drow = drow * inv
            wrow = wrow * inv
            for g in range(g0, groups):
                f = d[g][:, off + j : off + j + 1]
                if g == g0:
                    if r == 7:
                        continue
                    f = jnp.where(sub > r, f, 0.0)
                d[g] = d[g] - f * drow
                w[g] = w[g] - f * wrow
        scaled = []
        for g in range(groups):
            diag = jnp.sum(jnp.where(lane8 == sub8 + (off + 8 * g), d[g], 0.0), axis=1, keepdims=True)
            scaled.append(w[g] * lax.rsqrt(diag))
        wide = jnp.concatenate(scaled, axis=0)[:, :STEP]
        strip = dot(wide, work[top : top + STEP, :])
        work[top : top + STEP, :] = strip
        if top + STEP < PANEL:
            change = dot(strip[:, :PANEL], strip, ((0,), (0,)))
            work[top + STEP :, :] = work[top + STEP :, :] - change[top + STEP :, :]
    out_ref[...] = work[:, PANEL:]


def lower_inverse(left, right):
    return pl.pallas_call(
        invert_kernel,
        out_shape=jax.ShapeDtypeStruct((PANEL, PANEL), F32),
        scratch_shapes=[pltpu.VMEM((PANEL, 2 * PANEL), F32)],
        cost_estimate=pl.CostEstimate(flops=10**10, bytes_accessed=10**8, transcendentals=0),
        name="invert",
    )(left, right)


def pick_kernel(capacity, row_ids, col_ids, *refs):
    outs = refs[capacity:]
    for t in range(capacity):
        for m in range(col_ids.shape[0]):
            start = pl.multiple_of(col_ids[m] * BLOCK, BLOCK)
            outs[t * capacity + m % capacity][m // capacity] = refs[t][:, pl.ds(start, BLOCK)]


def pick_blocks(front, row_ids, col_ids, capacity):
    dests = row_ids.shape[0] // capacity
    ends = col_ids.shape[0] // capacity
    width = front.shape[1]

    def rows(t):
        return pl.BlockSpec((BLOCK, width), lambda i, r, c: (r[i * capacity + t], 0))

    return pl.pallas_call(
        functools.partial(pick_kernel, capacity),
        grid_spec=pltpu.PrefetchScalarGridSpec(
            num_scalar_prefetch=2,
            grid=(dests,),
            in_specs=[rows(t) for t in range(capacity)],
            out_specs=[
                pl.BlockSpec((None, ends, BLOCK, BLOCK), lambda i, r, c: (i, 0, 0, 0))
            ] * capacity**2,
        ),
        out_shape=[jax.ShapeDtypeStruct((dests, ends, BLOCK, BLOCK), F32)] * capacity**2,
        name="pick",
    )(row_ids, col_ids, *[front] * capacity)


def assemble_kernel(leaves, capacity, kblocks, rfrom, rok, rslot, cfrom, cok, parent_ref, *refs):
    squares = capacity**2
    blocks = refs[: leaves * squares]
    factors = refs[leaves * squares : leaves * (squares + 1)]
    uppers = refs[leaves * (squares + 1) : leaves * (squares + 2)]
    out_ref, high, low = refs[-3:]
    p = pl.program_id(0)
    steps = pl.num_programs(0)

    @pl.when(p == 0)
    def _():
        for s in range(leaves):
            high[s], low[s] = split(uppers[s][...])

    for k in range(kblocks):
        out_ref[:, k * BLOCK : (k + 1) * BLOCK] = parent_ref[pl.ds(k, BLOCK, stride=kblocks), :]
    for s in range(leaves):
        oks = [rok[(s * capacity + t) * steps + p] for t in range(capacity)]

        @pl.when(sum(oks) > 0)
        def _():
            parts = split(factors[s][...])
            for k in range(kblocks):
                m = cfrom[s * kblocks + k]

                @pl.when(cok[s * kblocks + k] > 0)
                def _():
                    start = pl.multiple_of(m * BLOCK, BLOCK)
                    cut = pl.ds(start, BLOCK)
                    value = -dot_split(parts, (high[s, :, cut], low[s, :, cut]))
                    for t in range(capacity):
                        for n in range(capacity):
                            take = (oks[t] > 0) & (m % capacity == n)
                            block = blocks[s * squares + t * capacity + n][m // capacity]
                            value = value + jnp.where(take, block, 0.0)
                    out_ref[:, k * BLOCK : (k + 1) * BLOCK] += value


def assemble(parent, pieces, factors, uppers, leaves, capacity, kblocks, tables):
    per_row = parent.shape[0] // (BLOCK * kblocks)
    ends = pieces[0].shape[1]
    width = uppers[0].shape[1]

    def piece_spec(n):
        place = n // capacity
        return pl.BlockSpec(
            (None, ends, BLOCK, BLOCK),
            lambda i, rf, *_: (rf[place * per_row + i], 0, 0, 0),
        )

    def factor_spec(s):
        return pl.BlockSpec(
            (BLOCK, PANEL), lambda i, rf, ro, rs, cf, co: (rs[s * per_row + i], 0)
        )

    return pl.pallas_call(
        functools.partial(assemble_kernel, leaves, capacity, kblocks),
        grid_spec=pltpu.PrefetchScalarGridSpec(
            num_scalar_prefetch=5,
            grid=(per_row,),
            in_specs=[pl.BlockSpec((BLOCK * kblocks, BLOCK), lambda i, *_: (i, 0))]
            + [piece_spec(n) for n in range(len(pieces))]
            + [factor_spec(s) for s in range(leaves)]
            + [pl.BlockSpec((PANEL, width), lambda i, *_: (0, 0))] * leaves,
            out_specs=pl.BlockSpec((BLOCK, kblocks * BLOCK), lambda i, *_: (i, 0)),
            scratch_shapes=[pltpu.VMEM((leaves, PANEL, width), jnp.bfloat16)] * 2,
        ),
        out_shape=jax.ShapeDtypeStruct((per_row * BLOCK, kblocks * BLOCK), F32),
        compiler_params=pltpu.CompilerParams(vmem_limit_bytes=48 * 2**20),
        name="assemble",
    )(*tables, parent, *pieces, *factors, *uppers)


def update_kernel(kblocks, lead, place, a_ref, p0_ref, p1_ref, inv_ref, top_ref, out_ref, ih, il, uh, ul):
    p = pl.program_id(0)
    rows = a_ref.shape[0]

    @pl.when(p == 0)
    def _():
        ih[...], il[...] = split(inv_ref[...].T)
        uh[...], ul[...] = split(dot(inv_ref[...], top_ref[...]))

    factor = dot_split(split(p0_ref[...]), (ih[:BLOCK], il[:BLOCK]))
    factor = factor + dot_split(split(p1_ref[...]), (ih[BLOCK:], il[BLOCK:]))
    parts = split(factor)
    line = lax.broadcasted_iota(jnp.int32, (rows, BLOCK), 0) + p * rows
    keep = (place[0] == 0) & (line < lead * BLOCK)
    for k in range(kblocks):
        span = slice(k * BLOCK, (k + 1) * BLOCK)
        mine = a_ref[:, span]
        value = jnp.where(keep, mine, mine - dot_split(parts, (uh[:, span], ul[:, span])))
        if k == 0:
            for block in range(lead):
                piece = factor[:, block * BLOCK : (block + 1) * BLOCK]
                value = jnp.where(place[1] == block, piece, value)
        out_ref[pl.ds(k, rows, stride=kblocks), :] = value


def update(assembled, panel0, panel1, inverse, top, place, kblocks):
    rows, width = assembled.shape
    tall = 2 * PANEL
    return pl.pallas_call(
        functools.partial(update_kernel, kblocks, PANEL // BLOCK),
        grid_spec=pltpu.PrefetchScalarGridSpec(
            num_scalar_prefetch=1,
            grid=(rows // tall,),
            in_specs=[
                pl.BlockSpec((tall, width), lambda i, _: (i, 0)),
                pl.BlockSpec((tall, BLOCK), lambda i, _: (i, 0)),
                pl.BlockSpec((tall, BLOCK), lambda i, _: (i, 0)),
                pl.BlockSpec((PANEL, PANEL), lambda i, _: (0, 0)),
                pl.BlockSpec((PANEL, width), lambda i, _: (0, 0)),
            ],
            out_specs=pl.BlockSpec((tall * kblocks, BLOCK), lambda i, _: (i, 0)),
            scratch_shapes=[pltpu.VMEM((PANEL, PANEL), jnp.bfloat16)] * 2
            + [pltpu.VMEM((PANEL, width), jnp.bfloat16)] * 2,
        ),
        out_shape=jax.ShapeDtypeStruct((rows * kblocks, BLOCK), F32),
        compiler_params=pltpu.CompilerParams(vmem_limit_bytes=40 * 2**20),
        name="update",
    )(place, assembled, panel0, panel1, inverse, top)


def ranks(targets, usable):
    count = targets.shape[-1]
    same = (targets[..., :, None] == targets[..., None, :]) & usable[..., None, :]
    before = jnp.arange(count)[None, :] < jnp.arange(count)[:, None]
    return jnp.sum(same & before, axis=-1)


def per_device(child_front, parent_front, block_map):
    front = child_front[0]
    grid_rows = lax.axis_size("row")
    grid_cols = lax.axis_size("col")
    leaves = lax.axis_size("leaf")
    row_id = lax.axis_index("row")
    col_id = lax.axis_index("col")
    leaf_id = lax.axis_index("leaf")
    blocks = front.shape[0] // BLOCK
    capacity = max(1, blocks // grid_rows)
    parent_rows, kblocks = parent_front.shape[:2]
    per_row = parent_rows // BLOCK
    period = leaves * grid_cols
    lead = PANEL // BLOCK

    padded = jnp.concatenate([jnp.full((leaves, lead), -1, jnp.int32), block_map], axis=1)
    maps = padded.reshape(leaves, grid_rows, blocks)
    usable = maps >= 0
    to_row = jnp.where(usable, maps // per_row, -1)
    to_col = jnp.where(usable, maps % grid_cols, -1)
    row_rank = ranks(to_row, usable)
    col_rank = ranks(to_col, usable)
    positions = jnp.arange(blocks)

    def picks(target, rank, group, count):
        target = target[leaf_id, group]
        rank = rank[leaf_id, group]
        chosen = (target == jnp.arange(count)[:, None, None]) & (
            rank == jnp.arange(capacity)[None, :, None]
        )
        return jnp.sum(jnp.where(chosen, positions, 0), axis=-1).astype(jnp.int32)

    row_ids = picks(to_row, row_rank, row_id, grid_rows)
    col_ids = picks(to_col, col_rank, col_id, grid_cols).reshape(-1)

    row_list = row_ids.reshape(-1)
    sends = pick_blocks(front, row_list, col_ids, capacity)

    corner = spread(spread(front[:PANEL, :PANEL], "row", 1), "col", 1)
    panel = spread(front[:, :PANEL], "col", 1)

    own_map = maps[leaf_id]
    corner_at = []
    for group_id in (row_id, col_id):
        for block in range(lead):
            found = own_map[group_id] == block
            corner_at.append((jnp.sum(jnp.where(found, positions, 0)), jnp.any(found)))
    rows_at, cols_at = corner_at[:lead], corner_at[lead:]

    def cut(x, i, j, wide, ok):
        block = lax.dynamic_slice(x, (i * BLOCK, j * BLOCK), (BLOCK, wide))
        return jnp.where(ok, block, 0.0)

    parent_flat = parent_front.reshape(parent_rows, kblocks, BLOCK)
    device = leaf_id * grid_cols + col_id
    raw = jnp.block(
        [[cut(front, i, j, BLOCK, a & b) for j, b in cols_at] for i, a in rows_at]
    )
    first = parent_flat[:PANEL, 0, :]
    raw = raw + jnp.concatenate(
        [jnp.where((row_id == 0) & (device == block), first, 0.0) for block in range(lead)], axis=1
    )
    touched = jnp.concatenate(
        [cut(front, i, 0, PANEL, a & (col_id == 0)) for i, a in rows_at], axis=0
    )
    raw, touched = lax.psum((raw, touched), ("row", "col"))

    order = (leaf_id - jnp.arange(leaves)) % leaves
    maps_here = maps[order]
    row_rank_here = row_rank[order]
    col_rank_here = col_rank[order]
    group = jnp.arange(grid_rows)[None, None, :, None]
    hit = maps_here[:, None] == (row_id * per_row + jnp.arange(per_row))[None, :, None, None]
    in_chunk = row_rank_here[:, None, None] == jnp.arange(capacity)[None, :, None, None, None]
    hit_chunk = hit[:, None] & in_chunk
    rfrom = jnp.sum(jnp.where(hit_chunk, group[:, None], 0), axis=(-1, -2))
    rok = jnp.sum(hit_chunk, axis=(-1, -2))
    slot = group * capacity + row_rank_here[:, None]
    rslot = jnp.sum(jnp.where(hit, slot, 0), axis=(-1, -2))
    owned = jnp.arange(kblocks) * period + device
    hit = maps_here[:, None] == owned[None, :, None, None]
    slot = group * capacity + col_rank_here[:, None]
    cfrom = jnp.sum(jnp.where(hit, slot, 0), axis=(-1, -2))
    cok = jnp.sum(hit, axis=(-1, -2))
    tables = [x.reshape(-1).astype(jnp.int32) for x in (rfrom, rok, rslot, cfrom, cok)]

    def exchange(x):
        return lax.all_to_all(x, ("row", "col"), split_axis=0, concat_axis=0, tiled=True)

    def leaf_copies(x):
        pairs = lambda shift: [(i, (i + shift) % leaves) for i in range(leaves)]
        return [x] + [lax.ppermute(x, "leaf", pairs(shift)) for shift in range(1, leaves)]

    by_block = panel.reshape(blocks, BLOCK, PANEL)
    picked = jnp.take(by_block, row_list, axis=0).reshape(grid_rows, capacity, BLOCK, PANEL)
    mine_cols = picks(to_col, col_rank, row_id, grid_cols)[col_id]
    for_cols = jnp.take(by_block, mine_cols, axis=0)
    packed = jnp.concatenate(
        [picked, jnp.broadcast_to(for_cols[None], (grid_rows, *for_cols.shape))], axis=1
    )

    inverse = lower_inverse(corner[:, :BLOCK], corner[:, BLOCK:])
    factor = dot(panel, inverse, ((1,), (1,)))
    half = dot(touched, inverse, ((1,), (1,)))
    corner_parent = lax.psum(raw - dot(half, half, ((1,), (1,))), "leaf")
    inverse_parent = lower_inverse(corner_parent[:, :BLOCK], corner_parent[:, BLOCK:])

    pieces = [[] for _ in range(leaves)]
    for out in sends:
        got = exchange(out.reshape(grid_rows * grid_cols, BLOCK, BLOCK))
        for shift, moved in enumerate(leaf_copies(got)):
            pieces[shift].append(moved.reshape(grid_rows, grid_cols, BLOCK, BLOCK))
    pieces = [x for part in pieces for x in part]
    got = lax.all_to_all(packed, "row", split_axis=0, concat_axis=0, tiled=True)
    factors, uppers = [], []
    for rows, inv in zip(leaf_copies(got), leaf_copies(inverse)):
        slots = grid_rows * capacity
        factors.append(dot(rows[:, :capacity].reshape(slots * BLOCK, PANEL), inv, ((1,), (1,))))
        uppers.append(dot(inv, rows[:, capacity:].reshape(slots * BLOCK, PANEL), ((1,), (1,))))
    assembled = assemble(
        parent_front.reshape(parent_rows * kblocks, BLOCK),
        pieces, factors, uppers, leaves, capacity, kblocks, tables,
    )

    panel = assembled[:, :BLOCK]
    middle = parent_rows // 2
    upper_half = spread(spread(panel[:middle], "col", 2), "leaf", 1)
    lower_half = spread(spread(panel[middle:], "leaf", 1), "col", 2)
    top = spread(assembled[:PANEL], "row", 1)
    panel0, panel1 = swap_pairs(jnp.concatenate([upper_half, lower_half], axis=0))
    place = jnp.stack([row_id, device]).astype(jnp.int32)
    result = update(assembled, panel0, panel1, inverse_parent, top, place, kblocks)
    return factor[None], result.reshape(parent_front.shape)


def solution(mesh):
    placed = (P("leaf", "row", "col"), P("row", None, ("leaf", "col"), None), P())
    return jax.shard_map(
        per_device,
        mesh=mesh,
        in_specs=placed,
        out_specs=(P("leaf", "row", None), P("row", None, ("leaf", "col"), None)),
        check_vma=False,
    )
```

time: 402 us -> 486 us (1.21)
  blocking collectives: 0 us -> 32.2 us
  local copies, waits for them, and re-layouts: 12 us -> 35.6 us
  between operations: 1.03 us -> 23.5 us
  Pallas kernels: 112 us -> 97.2 us
  waiting for transfers between devices: 178 us -> 164 us
  starting transfers between devices: 76.4 us -> 89.8 us
  other arithmetic: 10.3 us -> 23.2 us
  matrix products: 5.94 us -> 13.6 us
    all_to_all x2 -> x4, waiting for transfers between devices: 74.2 us -> 12.4 us  [the longest x3 12.4 us: exchange(): lax.all_to_all(x, ('row', 'col'), split_axis=0, concat_axis=0, tiled=True)]
    ppermute x2 -> x6, waiting for transfers between devices: 47.7 us -> 101 us  [leaf_copies(): lax.ppermute(x, 'leaf', pairs(shift))]
    all_to_all x0 -> x1, blocking collectives: none -> 32.2 us  [exchange(): lax.all_to_all(x, ('row', 'col'), split_axis=0, concat_axis=0, tiled=True)]
    all_to_all x2 -> x4, starting transfers between devices: 16 us -> 35.2 us  [the longest x3 28.9 us: exchange(): lax.all_to_all(x, ('row', 'col'), split_axis=0, concat_axis=0, tiled=True)]
    pallas_call x1, Pallas kernels: 32.2 us -> 15 us  [update(): pl.pallas_call(functools.partial(update_kernel, kblocks, PANEL // BLOCK),...]
    unnamed x0 -> x13, local copies, waits for them, and re-layouts: none -> 13.6 us
    ppermute x16 -> x12, waiting for transfers between devices: 55.6 us -> 43.2 us  [spread(): got = lax.ppermute(x, axis, pairs)]
    ppermute x16 -> x12, starting transfers between devices: 57.1 us -> 47.5 us  [spread(): got = lax.ppermute(x, axis, pairs)]
  transfers between devices with their start and end apart: 22 -> 25, of which waited for: 15 -> 10; matrix products, arithmetic and copies ran while one was open for 5% -> 13% of each run, Pallas kernels for 15% -> 16%
where the time goes in v2:
time: 486 us; the launch traced here: 479 us
  waiting for transfers between devices  164 us (34%)
  Pallas kernels  97.2 us (20%)
  starting transfers between devices  89.8 us (18%)
  local copies, waits for them, and re-layouts  35.6 us (7%)
  blocking collectives  32.2 us (7%)
  between operations  23.5 us (5%)
  other arithmetic  23.2 us (5%)
  matrix products  13.6 us (3%)
    ppermute x6, waiting for transfers between devices, leaf_copies(): lax.ppermute(x, 'leaf', pairs(shift))  101 us
    pallas_call x2, Pallas kernels, lower_inverse(): pl.pallas_call(invert_kernel, out_shape=jax.ShapeDtypeStruct((PANEL, PANE...  51.2 us
    ppermute x12, starting transfers between devices, spread(): got = lax.ppermute(x, axis, pairs)  47.5 us
    ppermute x12, waiting for transfers between devices, spread(): got = lax.ppermute(x, axis, pairs)  43.2 us
    all_to_all x1, blocking collectives, exchange(): lax.all_to_all(x, ('row', 'col'), split_axis=0, concat_axis=0, tiled=True)  32.2 us
    all_to_all x3, starting transfers between devices, exchange(): lax.all_to_all(x, ('row', 'col'), split_axis=0, concat_axis=0, tiled=True)  28.9 us
    pallas_call x1, Pallas kernels, assemble(): pl.pallas_call(functools.partial(assemble_kernel, leaves, capacity, kbloc...  25.6 us
    pallas_call x1, Pallas kernels, update(): pl.pallas_call(functools.partial(update_kernel, kblocks, PANEL // BLOCK),...  15 us
  transfers between devices with their start and end apart: 25, of which 10 were waited for; matrix products, arithmetic and copies ran while one was open for 13% of the time, Pallas kernels for 16%

profile of v2, /device:TPU:0, one launch (start us, length us, event | category | flops | bytes accessed | tf_op | source)
XLA Modules:
  0.0 479.3 jit_solution(15820359847201807491)
XLA Ops:
  10.3 5.5 %pick.1 = (f32[4,4,128,128]{3,2,1,0:T(8,128)}, f32[4,4,128,128]{3,2,1,0:T(8,128)}, f32[4,4,128,128]{3,2,1,0:T(8,128)}, f32[4,4,128,128]{3,2,1,0:T(8,128)}) custom-call(s32[8]{0:T(128)} %reshape.573.row_ids, s32[8]{0:T(128)} %reshape.574.col_ids, f32[1024,1024]{1,0:T(8,128)} %bitcast.100, f32[1024,1024]{1,0:T(8,128)} %bitcast.101), custom_call_target="tpu_custom_call" | custom-call | tf_op jit(solution)/shard_map/pick/pallas_call | solution.py:125
  15.8 32.2 %all_to_all.25 = f32[16,128,128]{2,1,0:T(8,128)S(1)} all-to-all(f32[16,128,128]{2,1,0:T(8,128)} %bitcast.119), channel_id=1, replica_groups=mesh['leaf'=2,'row'=4,'col'=4] {'row','col'}, dimensions={0} | all-to-all | bytes 2097152 | tf_op jit(solution)/shard_map/all_to_all | solution.py:357
  48.0 5.0 %all-to-all-start.1 = ((f32[16,128,128]{2,1,0:T(8,128)}), f32[16,128,128]{2,1,0:T(8,128)S(1)}, u32[]{:S(2)}, u32[]{:S(2)}) async-start(f32[16,128,128]{2,1,0:T(8,128)} %bitcast.118), calls=%async_computation.1 | async-start | bytes 2097152 | tf_op jit(solution)/shard_map/all_to_all | solution.py:357
  53.0 2.3 slice.69
  55.3 3.9 collective-permute-start
  59.2 19.2 %collective-permute-done = f32[1024,256]{1,0:T(8,128)S(1)} collective-permute-done((f32[1024,256]{1,0:T(8,128)}, f32[1024,256]{1,0:T(8,128)S(1)}, u32[]{:S(2)}, u32[]{:S(2)}) %collective-permute-start) | collective-permute-done | bytes 1048608 | tf_op jit(solution)/shard_map/ppermute | solution.py:39
  78.5 2.4 broadcast_select_fusion.5
  80.8 2.3 collective-permute-start.1
  83.2 5.5 %all-to-all-start.2 = ((f32[16,128,128]{2,1,0:T(8,128)}), f32[16,128,128]{2,1,0:T(8,128)S(1)}, u32[]{:S(2)}, u32[]{:S(2)}) async-start(f32[16,128,128]{2,1,0:T(8,128)} %bitcast.117), calls=%async_computation.2 | async-start | bytes 2097152 | tf_op jit(solution)/shard_map/all_to_all | solution.py:357
  89.2 2.3 broadcast_select_fusion.6
  91.5 2.8 gather_fusion.3
  94.3 1.8 gather_fusion.4
  96.2 1.4 broadcast_select_fusion
  97.7 1.5 pad_maximum_fusion
  99.2 12.4 %all-to-all-done.2 = f32[16,128,128]{2,1,0:T(8,128)S(1)} async-done(((f32[16,128,128]{2,1,0:T(8,128)}), f32[16,128,128]{2,1,0:T(8,128)S(1)}, u32[]{:S(2)}, u32[]{:S(2)}) %all-to-all-start.2) | async-done | bytes 1048608 | tf_op jit(solution)/shard_map/all_to_all | solution.py:357
  111.6 6.3 %all-to-all-start.4 = ((f32[4,4,128,256]{3,2,1,0:T(8,128)}), f32[4,4,128,256]{3,2,1,0:T(8,128)}, u32[]{:S(2)}, u32[]{:S(2)}) async-start(f32[4,4,128,256]{3,2,1,0:T(8,128)} %pad_maximum_fusion), calls=%async_computation.4 | async-start | bytes 4194304 | tf_op jit(solution)/shard_map/all_to_all | solution.py:383
  118.9 5.9 %collective-permute-start.2 = (f32[256,256]{1,0:T(8,128)S(1)}, f32[256,256]{1,0:T(8,128)}, u32[]{:S(2)}, u32[]{:S(2)}) collective-permute-start(f32[256,256]{1,0:T(8,128)S(1)} %slice.70), channel_id=1, source_target_pairs={{0,8},{1,9},{2,10},{3,11},{16,24},{17,25},{18,26},{19,27}} | collective-permute-start | bytes 786440 | tf_op jit(solution)/shard_map/ppermute | solution.py:39
  135.2 8.4 %copy.22 = f32[2048,8,1,128]{3,0,1,2:T(8,128)} copy(f32[2048,8,1,128]{3,2,1,0:T(1,128)} %param.4) | data formatting | bytes 16777216 | tf_op args[1]
  143.6 1.0 select_bitcast_fusion.1
  149.3 8.9 %collective-permute-done.2 = f32[256,256]{1,0:T(8,128)} collective-permute-done((f32[256,256]{1,0:T(8,128)S(1)}, f32[256,256]{1,0:T(8,128)}, u32[]{:S(2)}, u32[]{:S(2)}) %collective-permute-start.2) | collective-permute-done | bytes 262176 | tf_op jit(solution)/shard_map/ppermute | solution.py:39
  158.2 1.0 broadcast_select_fusion.12
  159.2 2.0 collective-permute-start.3
  161.9 4.1 collective-permute-done.3
  166.7 5.2 %collective-permute-start.4 = (f32[256,256]{1,0:T(8,128)}, f32[256,256]{1,0:T(8,128)}, u32[]{:S(2)}, u32[]{:S(2)}) collective-permute-start(f32[256,256]{1,0:T(8,128)} %broadcast_select_fusion.13), channel_id=1, source_target_pairs={{0,2},{4,6},{8,10},{12,14},{16,18},{20,22},{24,26},{28,30}} | collective-permute-start | bytes 786440 | tf_op jit(solution)/shard_map/ppermute | solution.py:39
  172.4 18.4 %all-to-all-start.3 = ((f32[16,128,128]{2,1,0:T(8,128)}), f32[16,128,128]{2,1,0:T(8,128)}, u32[]{:S(2)}, u32[]{:S(2)}) async-start(f32[16,128,128]{2,1,0:T(8,128)} %bitcast.116), calls=%async_computation.3 | async-start | bytes 2097152 | tf_op jit(solution)/shard_map/all_to_all | solution.py:357
  190.9 1.0 broadcast_select_fusion.14
  191.9 3.0 collective-permute-start.5
  195.1 1.5 collective-permute-start.10
  197.4 25.6 %invert.2 = f32[256,256]{1,0:T(8,128)} custom-call(f32[256,128]{1,0:T(8,128)} %get-tuple-element.57.left_ref, f32[256,128]{1,0:T(8,128)} %get-tuple-element.56.right_ref), custom_call_target="tpu_custom_call" | custom-call | flops 10000000000 | bytes 100000000 | tf_op jit(solution)/shard_map/invert/pallas_call | solution.py:100
  223.5 1.5 collective-permute-start.7
  225.5 1.5 collective-permute-start.9
  227.1 1.7 fusion.25
  228.8 2.0 fusion.30.refs_10_
  230.8 2.0 fusion.28.refs_8_
  232.8 11.3 %collective-permute-done.10 = f32[4,4,128,256]{3,2,1,0:T(8,128)} collective-permute-done((f32[4,4,128,256]{3,2,1,0:T(8,128)}, f32[4,4,128,256]{3,2,1,0:T(8,128)}, u32[]{:S(2)}, u32[]{:S(2)}) %collective-permute-start.10) | collective-permute-done | bytes 2097184 | tf_op jit(solution)/shard_map/ppermute | solution.py:361
  244.0 1.5 collective-permute-start.11
  245.5 1.7 fusion.24
  247.2 90.0 %collective-permute-done.11 = f32[256,256]{1,0:T(8,128)S(1)} collective-permute-done((f32[256,256]{1,0:T(8,128)S(1)}, f32[256,256]{1,0:T(8,128)S(1)}, u32[]{:S(2)}, u32[]{:S(2)}) %collective-permute-start.11) | collective-permute-done | bytes 262176 | tf_op jit(solution)/shard_map/ppermute | solution.py:361
  337.2 2.0 fusion.29.refs_9_
  339.3 2.1 fusion.31.refs_11_
  342.4 25.6 %assemble.1.a_ref = f32[2048,1024]{1,0:T(8,128)} custom-call(s32[64]{0:T(128)S(1)} %reshape.567.rfrom, s32[64]{0:T(128)S(1)} %reshape.568.rok, s32[32]{0:T(128)S(1)} %reshape.569.rslot, s32[16]{0:T(128)S(1)} %reshape.570.cfrom, s32[16]{0:T(128)S(1)} %reshape.571.cok, f32[16384,128]{1,0:T(8,128)} %bitcast.99, f32[4,4,128,128]{3,2,1,0:T(8,128)S(1)} %bitcast.96, ...), custom_call_target="tpu_custom_call" | custom-call | tf_op jit(solution)/shard_map/assemble/pallas_call | solution.py:195
  367.9 1.3 slice.82
  369.2 4.4 collective-permute-start.17
  373.6 2.2 fusion.23
  375.9 3.4 collective-permute-start.12
  379.3 4.2 collective-permute-start.14
  383.6 1.4 fusion.32
  384.9 2.1 convolution_subtract_fusion
  387.0 1.5 collective-permute-done.12
  389.3 4.7 collective-permute-done.14
  394.0 1.3 broadcast_select_fusion.8
  395.3 5.4 %collective-permute-start.13 = (f32[1024,128]{1,0:T(8,128)S(1)}, f32[1024,128]{1,0:T(8,128)}, u32[]{:S(2)}, u32[]{:S(2)}) collective-permute-start(f32[1024,128]{1,0:T(8,128)S(1)} %get-tuple-element.38), channel_id=1, source_target_pairs={{0,16},{1,17},{2,18},{3,19},{4,20},{5,21},{6,22},{7,23},{8,24},{9,... | collective-permute-start | bytes 1572872 | tf_op jit(solution)/shard_map/ppermute | solution.py:39
  400.7 7.3 %all-reduce.5.cloned.1.call-done = f32[256,256]{1,0:T(8,128)} async-done(((f32[256,256]{1,0:T(8,128)}), f32[256,256]{1,0:T(8,128)}) %all-reduce.5.cloned.1.call-update) | async-done | bytes 262160 | tf_op jit(solution)/shard_map/psum | solution.py:374
  408.0 1.7 fusion.26
  409.7 3.4 collective-permute-start.15
  413.1 1.4 broadcast_select_fusion.1
  414.5 4.4 collective-permute-start.18
  419.0 4.8 %collective-permute-done.15 = f32[1024,128]{1,0:T(8,128)S(1)} collective-permute-done((f32[1024,128]{1,0:T(8,128)S(1)}, f32[1024,128]{1,0:T(8,128)S(1)}, u32[]{:S(2)}, u32[]{:S(2)}) %collective-permute-start.15) | collective-permute-done | bytes 524320 | tf_op jit(solution)/shard_map/ppermute | solution.py:39
  423.8 1.1 pad_maximum_fusion.1
  424.9 25.7 %invert.3.inv_ref = f32[256,256]{1,0:T(8,128)} custom-call(f32[256,128]{1,0:T(8,128)} %get-tuple-element.55.left_ref, f32[256,128]{1,0:T(8,128)} %get-tuple-element.54.right_ref), custom_call_target="tpu_custom_call" | custom-call | flops 10000000000 | bytes 100000000 | tf_op jit(solution)/shard_map/invert/pallas_call | solution.py:100
  450.6 2.0 convolution_bitcast_fusion
  452.8 1.4 broadcast_select_fusion.3
  454.2 3.4 copy-done
  457.5 15.0 %update.1 = f32[16384,128]{1,0:T(8,128)} custom-call(s32[2]{0:T(128)S(1)} %pad_add_fusion.place, f32[2048,1024]{1,0:T(8,128)S(1)} %copy-done, f32[2048,128]{1,0:T(8,128)S(1)} %get-tuple-element.49.p0_ref, f32[2048,128]{1,0:T(8,128)S(1)} %get-tuple-element.48.p1_ref, f32[256,256]{1,0:T(8,128)S(1)} %copy-done.1, f32[256,1024]{1,0:T(8,128)S(1)} %broadcast_select_fusion.2.top_ref), custom_call_target="tpu_custom_call" | custom-call | tf_op jit(solution)/shard_map/update/pallas_call | solution.py:241
  (98 shorter events, 17.0 us)
Async XLA Ops:
  48.0 35.1 %all-to-all-start.1 = ((f32[16,128,128]{2,1,0:T(8,128)}), f32[16,128,128]{2,1,0:T(8,128)S(1)}, u32[]{:S(2)}, u32[]{:S(2)}) async-start(f32[16,128,128]{2,1,0:T(8,128)} %bitcast.118), calls=%async_computation.1 | async-start | bytes 2097152 | tf_op jit(solution)/shard_map/all_to_all | solution.py:357
  55.3 23.1 %collective-permute-start = (f32[1024,256]{1,0:T(8,128)}, f32[1024,256]{1,0:T(8,128)S(1)}, u32[]{:S(2)}, u32[]{:S(2)}) collective-permute-start(f32[1024,256]{1,0:T(8,128)} %slice.69), channel_id=1, source_target_pairs={{0,2},{4,6},{8,10},{12,14},{16,18},{20,22},{24,26},{28,30}} | collective-permute-start | bytes 3145736 | tf_op jit(solution)/shard_map/ppermute | solution.py:39
  80.8 8.3 %collective-permute-start.1 = (f32[1024,256]{1,0:T(8,128)}, f32[1024,256]{1,0:T(8,128)}, u32[]{:S(2)}, u32[]{:S(2)}) collective-permute-start(f32[1024,256]{1,0:T(8,128)} %broadcast_select_fusion.5), channel_id=1, source_target_pairs={{0,1},{2,3},{4,5},{6,7},{8,9},{10,11},{12,13},{14,15},{16,17},{18,... | collective-permute-start | bytes 3145736 | tf_op jit(solution)/shard_map/ppermute | solution.py:39
  83.2 28.5 %all-to-all-start.2 = ((f32[16,128,128]{2,1,0:T(8,128)}), f32[16,128,128]{2,1,0:T(8,128)S(1)}, u32[]{:S(2)}, u32[]{:S(2)}) async-start(f32[16,128,128]{2,1,0:T(8,128)} %bitcast.117), calls=%async_computation.2 | async-start | bytes 2097152 | tf_op jit(solution)/shard_map/all_to_all | solution.py:357
  111.6 60.8 %all-to-all-start.4 = ((f32[4,4,128,256]{3,2,1,0:T(8,128)}), f32[4,4,128,256]{3,2,1,0:T(8,128)}, u32[]{:S(2)}, u32[]{:S(2)}) async-start(f32[4,4,128,256]{3,2,1,0:T(8,128)} %pad_maximum_fusion), calls=%async_computation.4 | async-start | bytes 4194304 | tf_op jit(solution)/shard_map/all_to_all | solution.py:383
  118.0 265.6 %all-reduce.7.cloned.1.call-start = ((), (), s32[]{:S(2)}) async-start(), calls=%async_computation.6 | async-start | bytes 1048576 | tf_op jit(solution)/shard_map/psum | solution.py:335
  118.9 39.2 %collective-permute-start.2 = (f32[256,256]{1,0:T(8,128)S(1)}, f32[256,256]{1,0:T(8,128)}, u32[]{:S(2)}, u32[]{:S(2)}) collective-permute-start(f32[256,256]{1,0:T(8,128)S(1)} %slice.70), channel_id=1, source_target_pairs={{0,8},{1,9},{2,10},{3,11},{16,24},{17,25},{18,26},{19,27}} | collective-permute-start | bytes 786440 | tf_op jit(solution)/shard_map/ppermute | solution.py:39
  159.2 6.8 %collective-permute-start.3 = (f32[256,256]{1,0:T(8,128)S(1)}, f32[256,256]{1,0:T(8,128)}, u32[]{:S(2)}, u32[]{:S(2)}) collective-permute-start(f32[256,256]{1,0:T(8,128)S(1)} %broadcast_select_fusion.12), channel_id=1, source_target_pairs={{0,4},{8,12},{1,5},{9,13},{2,6},{10,14},{3,7},{11,15},{16,20},{24,... | collective-permute-start | bytes 786440 | tf_op jit(solution)/shard_map/ppermute | solution.py:39
  166.7 24.2 %collective-permute-start.4 = (f32[256,256]{1,0:T(8,128)}, f32[256,256]{1,0:T(8,128)}, u32[]{:S(2)}, u32[]{:S(2)}) collective-permute-start(f32[256,256]{1,0:T(8,128)} %broadcast_select_fusion.13), channel_id=1, source_target_pairs={{0,2},{4,6},{8,10},{12,14},{16,18},{20,22},{24,26},{28,30}} | collective-permute-start | bytes 786440 | tf_op jit(solution)/shard_map/ppermute | solution.py:39
  172.4 53.1 %all-to-all-start.3 = ((f32[16,128,128]{2,1,0:T(8,128)}), f32[16,128,128]{2,1,0:T(8,128)}, u32[]{:S(2)}, u32[]{:S(2)}) async-start(f32[16,128,128]{2,1,0:T(8,128)} %bitcast.116), calls=%async_computation.3 | async-start | bytes 2097152 | tf_op jit(solution)/shard_map/all_to_all | solution.py:357
  190.8 217.2 %all-reduce.5.cloned.1.call-start = ((), (), s32[]{:S(2)}) async-start(), calls=%async_computation.5 | async-start | bytes 524288 | tf_op jit(solution)/shard_map/psum | solution.py:374
  191.9 4.8 collective-permute-start.5
  195.1 48.9 %collective-permute-start.10 = (f32[4,4,128,256]{3,2,1,0:T(8,128)}, f32[4,4,128,256]{3,2,1,0:T(8,128)}, u32[]{:S(2)}, u32[]{:S(2)}) collective-permute-start(f32[4,4,128,256]{3,2,1,0:T(8,128)} %all-to-all-done.4), channel_id=1, source_target_pairs={{0,16},{16,0},{1,17},{17,1},{2,18},{18,2},{3,19},{19,3},{4,20},{20... | collective-permute-start | bytes 6291464 | tf_op jit(solution)/shard_map/ppermute | solution.py:361
  223.0 5.7 %copy-start.3 = (f32[256,256]{1,0:T(8,128)S(1)}, f32[256,256]{1,0:T(8,128)}, u32[]{:S(2)}) copy-start(f32[256,256]{1,0:T(8,128)} %invert.2) | copy-start | bytes 786436
  223.0 118.4 %collective-permute-start.6 = (f32[16,128,128]{2,1,0:T(8,128)S(1)}, f32[16,128,128]{2,1,0:T(8,128)}, u32[]{:S(2)}, u32[]{:S(2)}) collective-permute-start(f32[16,128,128]{2,1,0:T(8,128)S(1)} %all_to_all.25), channel_id=1, source_target_pairs={{0,16},{16,0},{1,17},{17,1},{2,18},{18,2},{3,19},{19,3},{4,20},{20... | collective-permute-start | bytes 3145736 | tf_op jit(solution)/shard_map/ppermute | solution.py:361
  223.5 117.9 %collective-permute-start.7 = (f32[16,128,128]{2,1,0:T(8,128)S(1)}, f32[16,128,128]{2,1,0:T(8,128)}, u32[]{:S(2)}, u32[]{:S(2)}) collective-permute-start(f32[16,128,128]{2,1,0:T(8,128)S(1)} %all-to-all-done.1), channel_id=1, source_target_pairs={{0,16},{16,0},{1,17},{17,1},{2,18},{18,2},{3,19},{19,3},{4,20},{20... | collective-permute-start | bytes 3145736 | tf_op jit(solution)/shard_map/ppermute | solution.py:361
  225.0 116.3 %collective-permute-start.8 = (f32[16,128,128]{2,1,0:T(8,128)S(1)}, f32[16,128,128]{2,1,0:T(8,128)}, u32[]{:S(2)}, u32[]{:S(2)}) collective-permute-start(f32[16,128,128]{2,1,0:T(8,128)S(1)} %all-to-all-done.2), channel_id=1, source_target_pairs={{0,16},{16,0},{1,17},{17,1},{2,18},{18,2},{3,19},{19,3},{4,20},{20... | collective-permute-start | bytes 3145736 | tf_op jit(solution)/shard_map/ppermute | solution.py:361
  225.5 115.8 %collective-permute-start.9 = (f32[16,128,128]{2,1,0:T(8,128)}, f32[16,128,128]{2,1,0:T(8,128)S(1)}, u32[]{:S(2)}, u32[]{:S(2)}) collective-permute-start(f32[16,128,128]{2,1,0:T(8,128)} %all-to-all-done.3), channel_id=1, source_target_pairs={{0,16},{16,0},{1,17},{17,1},{2,18},{18,2},{3,19},{19,3},{4,20},{20... | collective-permute-start | bytes 3145736 | tf_op jit(solution)/shard_map/ppermute | solution.py:361
  244.0 93.2 %collective-permute-start.11 = (f32[256,256]{1,0:T(8,128)S(1)}, f32[256,256]{1,0:T(8,128)S(1)}, u32[]{:S(2)}, u32[]{:S(2)}) collective-permute-start(f32[256,256]{1,0:T(8,128)S(1)} %copy-done.3), channel_id=1, source_target_pairs={{0,16},{16,0},{1,17},{17,1},{2,18},{18,2},{3,19},{19,3},{4,20},{20... | collective-permute-start | bytes 786440 | tf_op jit(solution)/shard_map/ppermute | solution.py:361
  341.4 1.0 copy-start.4
  369.2 43.9 %collective-permute-start.17 = (f32[256,1024]{1,0:T(8,128)S(1)}, f32[256,1024]{1,0:T(8,128)S(1)}, u32[]{:S(2)}, u32[]{:S(2)}) collective-permute-start(f32[256,1024]{1,0:T(8,128)S(1)} %slice.82), channel_id=1, source_target_pairs={{0,8},{1,9},{2,10},{3,11},{16,24},{17,25},{18,26},{19,27}} | collective-permute-start | bytes 3145736 | tf_op jit(solution)/shard_map/ppermute | solution.py:39
  375.9 12.6 %collective-permute-start.12 = (f32[1024,128]{1,0:T(8,128)}, f32[1024,128]{1,0:T(8,128)S(1)}, u32[]{:S(2)}, u32[]{:S(2)}) collective-permute-start(f32[1024,128]{1,0:T(8,128)} %get-tuple-element.40), channel_id=1, source_target_pairs={{0,2},{1,3},{4,6},{5,7},{8,10},{9,11},{12,14},{13,15},{16,18},{17,... | collective-permute-start | bytes 1572872 | tf_op jit(solution)/shard_map/ppermute | solution.py:39
  379.3 14.7 %collective-permute-start.14 = (f32[1024,128]{1,0:T(8,128)}, f32[1024,128]{1,0:T(8,128)}, u32[]{:S(2)}, u32[]{:S(2)}) collective-permute-start(f32[1024,128]{1,0:T(8,128)} %get-tuple-element.41), channel_id=1, source_target_pairs={{0,16},{1,17},{2,18},{3,19},{4,20},{5,21},{6,22},{7,23},{8,24},{9,... | collective-permute-start | bytes 1572872 | tf_op jit(solution)/shard_map/ppermute | solution.py:39
  388.5 0.8 copy-start.5
  395.3 23.5 %collective-permute-start.13 = (f32[1024,128]{1,0:T(8,128)S(1)}, f32[1024,128]{1,0:T(8,128)}, u32[]{:S(2)}, u32[]{:S(2)}) collective-permute-start(f32[1024,128]{1,0:T(8,128)S(1)} %get-tuple-element.38), channel_id=1, source_target_pairs={{0,16},{1,17},{2,18},{3,19},{4,20},{5,21},{6,22},{7,23},{8,24},{9,... | collective-permute-start | bytes 1572872 | tf_op jit(solution)/shard_map/ppermute | solution.py:39
  409.7 14.1 %collective-permute-start.15 = (f32[1024,128]{1,0:T(8,128)S(1)}, f32[1024,128]{1,0:T(8,128)S(1)}, u32[]{:S(2)}, u32[]{:S(2)}) collective-permute-start(f32[1024,128]{1,0:T(8,128)S(1)} %get-tuple-element.39), channel_id=1, source_target_pairs={{0,2},{1,3},{4,6},{5,7},{8,10},{9,11},{12,14},{13,15},{16,18},{17,... | collective-permute-start | bytes 1572872 | tf_op jit(solution)/shard_map/ppermute | solution.py:39
  414.5 38.1 %collective-permute-start.18 = (f32[256,1024]{1,0:T(8,128)S(1)}, f32[256,1024]{1,0:T(8,128)}, u32[]{:S(2)}, u32[]{:S(2)}) collective-permute-start(f32[256,1024]{1,0:T(8,128)S(1)} %broadcast_select_fusion.1), channel_id=1, source_target_pairs={{0,4},{8,12},{1,5},{9,13},{2,6},{10,14},{3,7},{11,15},{16,20},{24,... | collective-permute-start | bytes 3145736 | tf_op jit(solution)/shard_map/ppermute | solution.py:39
  424.9 27.8 %collective-permute-start.16 = (f32[2048,128]{1,0:T(8,128)}, f32[2048,128]{1,0:T(8,128)}, u32[]{:S(2)}, u32[]{:S(2)}) collective-permute-start(f32[2048,128]{1,0:T(8,128)} %pad_maximum_fusion.1), channel_id=1, source_target_pairs={{0,1},{1,0},{2,3},{3,2},{4,5},{5,4},{6,7},{7,6},{8,9},{9,8},{10,11... | collective-permute-start | bytes 3145736 | tf_op jit(solution)/shard_map/ppermute | solution.py:49
  424.9 25.7 %copy-start.2 = (f32[1024,256]{1,0:T(8,128)S(1)}, f32[1024,256]{1,0:T(8,128)}, u32[]{:S(2)}) copy-start(f32[1024,256]{1,0:T(8,128)} %broadcast_select_fusion.6) | copy-start | bytes 3145732
  452.6 1.6 copy-start.1
  454.2 3.4 copy-start
Sparse Core Ops, SparseCore 0:
  148.1 104.4 all-reduce.6
  387.1 20.8 all-reduce.4

commit v3 on v1

--- a/solution.py
+++ b/solution.py
@@ -16,6 +16,16 @@
 
 def dot(left, right, dims=((1,), (0,))):
     return lax.dot_general(left, right, (dims, ((), ())), precision=HIGH, preferred_element_type=F32)
+
+
+def split(x):
+    high = x.astype(jnp.bfloat16)
+    return high, (x - high.astype(F32)).astype(jnp.bfloat16)
+
+
+def dot_split(left, right):
+    one = lambda a, b: jnp.dot(a, b, preferred_element_type=F32)
+    return one(left[0], right[0]) + (one(left[0], right[1]) + one(left[1], right[0]))
 
 
 def spread(x, axis, unit):
@@ -166,45 +176,52 @@
     )(rfrom, rok, cfrom, cok, parent, *pieces)
 
 
-def update_kernel(kblocks, lead, place, a_ref, p0_ref, p1_ref, inv_ref, top_ref, out_ref, upper):
+def update_kernel(kblocks, lead, place, a_ref, p0_ref, p1_ref, inv_ref, top_ref, out_ref, ih, il, uh, ul):
     p = pl.program_id(0)
+    rows = a_ref.shape[0]
 
     @pl.when(p == 0)
     def _():
-        upper[...] = dot(inv_ref[...], top_ref[...])
-
-    factor = dot(p0_ref[...], inv_ref[:, :BLOCK], ((1,), (1,)))
-    factor = factor + dot(p1_ref[...], inv_ref[:, BLOCK:], ((1,), (1,)))
-    keep = (place[0] == 0) & (p < lead)
+        ih[...], il[...] = split(inv_ref[...].T)
+        uh[...], ul[...] = split(dot(inv_ref[...], top_ref[...]))
+
+    factor = dot_split(split(p0_ref[...]), (ih[:BLOCK], il[:BLOCK]))
+    factor = factor + dot_split(split(p1_ref[...]), (ih[BLOCK:], il[BLOCK:]))
+    parts = split(factor)
+    line = lax.broadcasted_iota(jnp.int32, (rows, BLOCK), 0) + p * rows
+    keep = (place[0] == 0) & (line < lead * BLOCK)
     for k in range(kblocks):
         span = slice(k * BLOCK, (k + 1) * BLOCK)
         mine = a_ref[:, span]
-        value = jnp.where(keep, mine, mine - dot(factor, upper[:, span]))
+        value = jnp.where(keep, mine, mine - dot_split(parts, (uh[:, span], ul[:, span])))
         if k == 0:
             for block in range(lead):
                 piece = factor[:, block * BLOCK : (block + 1) * BLOCK]
                 value = jnp.where(place[1] == block, piece, value)
-        out_ref[pl.ds(k, BLOCK, stride=kblocks), :] = value
+        out_ref[pl.ds(k, rows, stride=kblocks), :] = value
 
 
 def update(assembled, panel0, panel1, inverse, top, place, kblocks):
     rows, width = assembled.shape
+    tall = 2 * PANEL
     return pl.pallas_call(
         functools.partial(update_kernel, kblocks, PANEL // BLOCK),
         grid_spec=pltpu.PrefetchScalarGridSpec(
             num_scalar_prefetch=1,
-            grid=(rows // BLOCK,),
+            grid=(rows // tall,),
             in_specs=[
-                pl.BlockSpec((BLOCK, width), lambda i, _: (i, 0)),
-                pl.BlockSpec((BLOCK, BLOCK), lambda i, _: (i, 0)),
-                pl.BlockSpec((BLOCK, BLOCK), lambda i, _: (i, 0)),
+                pl.BlockSpec((tall, width), lambda i, _: (i, 0)),
+                pl.BlockSpec((tall, BLOCK), lambda i, _: (i, 0)),
+                pl.BlockSpec((tall, BLOCK), lambda i, _: (i, 0)),
                 pl.BlockSpec((PANEL, PANEL), lambda i, _: (0, 0)),
                 pl.BlockSpec((PANEL, width), lambda i, _: (0, 0)),
             ],
-            out_specs=pl.BlockSpec((BLOCK * kblocks, BLOCK), lambda i, _: (i, 0)),
-            scratch_shapes=[pltpu.VMEM((PANEL, width), F32)],
+            out_specs=pl.BlockSpec((tall * kblocks, BLOCK), lambda i, _: (i, 0)),
+            scratch_shapes=[pltpu.VMEM((PANEL, PANEL), jnp.bfloat16)] * 2
+            + [pltpu.VMEM((PANEL, width), jnp.bfloat16)] * 2,
         ),
         out_shape=jax.ShapeDtypeStruct((rows * kblocks, BLOCK), F32),
+        compiler_params=pltpu.CompilerParams(vmem_limit_bytes=40 * 2**20),
         name="update",
     )(place, assembled, panel0, panel1, inverse, top)
 
@@ -232,11 +249,8 @@
     lead = PANEL // BLOCK
 
     corner = spread(spread(front[:PANEL, :PANEL], "row", 1), "col", 1)
-    corner, panel_rows, top_rows = lax.optimization_barrier(
-        (corner, front[:, :PANEL], front[:PANEL, :])
-    )
-    panel_rows = spread(panel_rows, "col", 1)
-    top_rows = spread(top_rows, "row", 1)
+    top_rows = spread(front[:PANEL, :], "row", 1)
+    panel_rows = spread(front[:, :PANEL], "col", 1)
     inverse = lower_inverse(corner[:, :BLOCK], corner[:, BLOCK:])
 
     padded = jnp.concatenate([jnp.full((leaves, lead), -1, jnp.int32), block_map], axis=1)
@@ -284,6 +298,31 @@
         out = out.reshape(grid_rows * grid_cols, capacity, BLOCK, BLOCK)
         got = lax.all_to_all(out, ("row", "col"), split_axis=0, concat_axis=0, tiled=True)
         own.append(got)
+    own_map = maps[leaf_id]
+    device = leaf_id * grid_cols + col_id
+
+    def place_of(group_id, block):
+        found = own_map[group_id] == block
+        return jnp.sum(jnp.where(found, positions, 0)), jnp.any(found)
+
+    rows_at = [place_of(row_id, block) for block in range(lead)]
+    cols_at = [place_of(col_id, block) for block in range(lead)]
+
+    def cut(x, i, j, shape, ok):
+        return jnp.where(ok, lax.dynamic_slice(x, (i * BLOCK, j * BLOCK), shape), 0.0)
+
+    square = (BLOCK, BLOCK)
+    share = jnp.block([[cut(front, i, j, square, a & b) for j, b in cols_at] for i, a in rows_at])
+    left = jnp.concatenate([cut(factor, i, 0, (BLOCK, PANEL), a) for i, a in rows_at], axis=0)
+    right = jnp.concatenate([cut(upper, 0, j, (PANEL, BLOCK), b) for j, b in cols_at], axis=1)
+    first = parent_front[:PANEL, 0, 0, :]
+    given = jnp.concatenate(
+        [jnp.where((row_id == 0) & (device == block), first, 0.0) for block in range(lead)], axis=1
+    )
+    corner_parent = lax.psum(given + (share - dot(left, right)), ("leaf", "row", "col"))
+    corner_parent, own[-1] = lax.optimization_barrier((corner_parent, own[-1]))
+    inverse_parent = lower_inverse(corner_parent[:, :BLOCK], corner_parent[:, BLOCK:])
+
     pieces = [[] for _ in range(leaves)]
     for got in own:
         for shift in range(leaves):
@@ -295,20 +334,19 @@
                 moved.reshape(grid_rows, grid_cols * capacity, BLOCK, BLOCK)
             )
     pieces = [x for part in pieces for x in part]
+    inverse_parent, rok = lax.optimization_barrier((inverse_parent, rok))
     assembled = assemble(
         parent_front.reshape(parent_rows * kblocks, BLOCK),
         pieces, leaves, capacity, kblocks, rfrom, rok, cfrom, cok,
     )
 
-    piece = spread(spread(assembled[:PANEL, :BLOCK], "col", 2), "leaf", 1)
-    piece, panel = lax.optimization_barrier((piece, assembled[:, :BLOCK]))
-    panel = spread(spread(panel, "col", 2), "leaf", 1)
-    panel0, panel1 = swap_pairs(panel)
-    corner0, corner1 = swap_pairs(spread(piece, "row", 1))
-    corner0, corner1, top = lax.optimization_barrier((corner0, corner1, assembled[:PANEL]))
-    top = spread(top, "row", 1)
-    inverse_parent = lower_inverse(corner0, corner1)
-    place = jnp.stack([row_id, leaf_id * grid_cols + col_id]).astype(jnp.int32)
+    panel = assembled[:, :BLOCK]
+    middle = parent_rows // 2
+    upper_half = spread(spread(panel[:middle], "col", 2), "leaf", 1)
+    lower_half = spread(spread(panel[middle:], "leaf", 1), "col", 2)
+    top = spread(assembled[:PANEL], "row", 1)
+    panel0, panel1 = swap_pairs(jnp.concatenate([upper_half, lower_half], axis=0))
+    place = jnp.stack([row_id, device]).astype(jnp.int32)
     result = update(assembled, panel0, panel1, inverse_parent, top, place, kblocks)
     return factor[None], result.reshape(parent_front.shape)
 

time: 402 us -> 501 us (1.25)
  waiting for transfers between devices: 178 us -> 276 us
  between operations: 1.03 us -> 21.8 us
  Pallas kernels: 112 us -> 95.3 us
  starting transfers between devices: 76.4 us -> 63.5 us
  other arithmetic: 10.3 us -> 17.1 us
  local copies, waits for them, and re-layouts: 12 us -> 17.1 us
    psum x0 -> x1, waiting for transfers between devices: none -> 135 us  [per_device(): lax.psum(given + (share - dot(left, right)), ('leaf', 'row', 'col'))]
    all_to_all x2, waiting for transfers between devices: 74.2 us -> 34.7 us  [per_device(): lax.all_to_all(out, ('row', 'col'), split_axis=0, concat_axis=0, tiled=True)]
    pallas_call x1, Pallas kernels: 32.2 us -> 15.2 us  [update(): pl.pallas_call(functools.partial(update_kernel, kblocks, PANEL // BLOCK),...]
    ppermute x2, waiting for transfers between devices: 47.7 us -> 60.4 us  [per_device(): moved = lax.ppermute(got, 'leaf', pairs)]
    ppermute x16 -> x14, starting transfers between devices: 57.1 us -> 45.2 us  [spread(): got = lax.ppermute(x, axis, pairs)]
    ppermute x16 -> x14, waiting for transfers between devices: 55.6 us -> 45.8 us  [spread(): got = lax.ppermute(x, axis, pairs)]
    select_n x0 -> x4, other arithmetic: none -> 5.47 us  [the longest x3 5.45 us: cut(): jnp.where(ok, lax.dynamic_slice(x, (i * BLOCK, j * BLOCK), shape), 0.0)]
  transfers between devices with their start and end apart: 22 -> 20, of which waited for: 15 -> 10; matrix products, arithmetic and copies ran while one was open for 5% -> 7% of each run, Pallas kernels for 15% -> 12%
where the time goes in v3:
time: 501 us; the launch traced here: 498 us
  waiting for transfers between devices  276 us (55%)
  Pallas kernels  95.3 us (19%)
  starting transfers between devices  63.5 us (13%)
  between operations  21.8 us (4%)
  local copies, waits for them, and re-layouts  17.1 us (3%)
  other arithmetic  17.1 us (3%)
  matrix products  7.04 us (1%)
    psum x1, waiting for transfers between devices, per_device(): lax.psum(given + (share - dot(left, right)), ('leaf', 'row', 'col'))  135 us
    ppermute x2, waiting for transfers between devices, per_device(): moved = lax.ppermute(got, 'leaf', pairs)  60.4 us
    pallas_call x2, Pallas kernels, lower_inverse(): pl.pallas_call(invert_kernel, out_shape=jax.ShapeDtypeStruct((PANEL, PANE...  51.1 us
    ppermute x14, waiting for transfers between devices, spread(): got = lax.ppermute(x, axis, pairs)  45.8 us
    ppermute x14, starting transfers between devices, spread(): got = lax.ppermute(x, axis, pairs)  45.2 us
    all_to_all x2, waiting for transfers between devices, per_device(): lax.all_to_all(out, ('row', 'col'), split_axis=0, concat_axis=0, tiled=True)  34.7 us
    all_to_all x2, starting transfers between devices, per_device(): lax.all_to_all(out, ('row', 'col'), split_axis=0, concat_axis=0, tiled=True)  16.2 us
    pallas_call x1, Pallas kernels, assemble(): pl.pallas_call(functools.partial(assemble_kernel, leaves, capacity, kbloc...  16.1 us
  transfers between devices with their start and end apart: 20, of which 10 were waited for; matrix products, arithmetic and copies ran while one was open for 7% of the time, Pallas kernels for 12%

profile of v3, /device:TPU:0, one launch (start us, length us, event | category | flops | bytes accessed | tf_op | source)
XLA Modules:
  0.0 498.1 jit_solution(6135630995950846867)
XLA Ops:
  7.2 1.0 slice.66
  8.2 6.7 %collective-permute-start.2 = (f32[256,256]{1,0:T(8,128)S(1)}, f32[256,256]{1,0:T(8,128)}, u32[]{:S(2)}, u32[]{:S(2)}) collective-permute-start(f32[256,256]{1,0:T(8,128)S(1)} %slice.66), channel_id=1, source_target_pairs={{0,8},{1,9},{2,10},{3,11},{16,24},{17,25},{18,26},{19,27}} | collective-permute-start | bytes 786440 | tf_op jit(solution)/shard_map/ppermute | solution.py:39
  14.8 1.3 slice_bitcast_fusion
  16.1 2.3 collective-permute-start.6
  18.4 1.3 slice.65
  19.7 3.5 collective-permute-start
  23.4 0.4 convert_reduce_fusion
  23.9 1.0 broadcast_select_fusion.10
  25.0 2.0 collective-permute-start.3
  27.0 20.7 %collective-permute-done.3 = f32[256,256]{1,0:T(8,128)} collective-permute-done((f32[256,256]{1,0:T(8,128)S(1)}, f32[256,256]{1,0:T(8,128)}, u32[]{:S(2)}, u32[]{:S(2)}) %collective-permute-start.3) | collective-permute-done | bytes 262176 | tf_op jit(solution)/shard_map/ppermute | solution.py:39
  47.7 1.0 broadcast_select_fusion.11
  48.7 4.1 collective-permute-start.4
  53.1 0.6 reshape.392.col_ids
  53.7 0.6 slice_bitcast_fusion.1
  54.3 1.7 collective-permute-done.4
  56.0 1.3 collective-permute-start.5
  57.4 1.4 broadcast_select_fusion.3
  58.7 5.5 %collective-permute-start.7 = (f32[256,1024]{1,0:T(8,128)S(1)}, f32[256,1024]{1,0:T(8,128)}, u32[]{:S(2)}, u32[]{:S(2)}) collective-permute-start(f32[256,1024]{1,0:T(8,128)S(1)} %broadcast_select_fusion.3), channel_id=1, source_target_pairs={{0,4},{8,12},{1,5},{9,13},{2,6},{10,14},{3,7},{11,15},{16,20},{24,... | collective-permute-start | bytes 3145736 | tf_op jit(solution)/shard_map/ppermute | solution.py:39
  64.2 1.4 broadcast_select_fusion.5
  65.7 0.7 fusion.34
  66.4 1.3 collective-permute-start.1
  67.7 25.6 %invert.2 = f32[256,256]{1,0:T(8,128)} custom-call(f32[256,128]{1,0:T(8,128)} %get-tuple-element.49.left_ref, f32[256,128]{1,0:T(8,128)} %get-tuple-element.48.right_ref), custom_call_target="tpu_custom_call" | custom-call | flops 10000000000 | bytes 100000000 | tf_op jit(solution)/shard_map/invert/pallas_call | solution.py:100
  93.3 3.0 fusion.1.u_ref
  96.3 2.9 fusion.3.f_ref
  99.2 6.4 %schur.2 = f32[4,8,128,128]{3,2,1,0:T(8,128)} custom-call(s32[4]{0:T(128)} %get-tuple-element.58.row_ids, s32[8]{0:T(128)} %reshape.392.col_ids, f32[1024,1024]{1,0:T(8,128)} %bitcast.68, f32[1024,256]{1,0:T(8,128)} %fusion.3.f_ref, f32[256,1024]{1,0:T(8,128)} %fusion.1.u_ref), custom_call_target="tpu_custom_call" | custom-call | flops 1610612736 | bytes 4194304 | tf_op jit(solution)/shard_map/schur/pallas_call | solution.py:119
  105.7 4.9 all-to-all-start
  110.6 6.4 %schur.3 = f32[4,8,128,128]{3,2,1,0:T(8,128)} custom-call(s32[4]{0:T(128)} %get-tuple-element.57.row_ids, s32[8]{0:T(128)} %reshape.392.col_ids, f32[1024,1024]{1,0:T(8,128)} %bitcast.69, f32[1024,256]{1,0:T(8,128)} %fusion.3.f_ref, f32[256,1024]{1,0:T(8,128)} %fusion.1.u_ref), custom_call_target="tpu_custom_call" | custom-call | flops 1610612736 | bytes 4194304 | tf_op jit(solution)/shard_map/schur/pallas_call | solution.py:119
  117.0 34.7 %all-to-all-done = f32[16,2,128,128]{3,2,1,0:T(8,128)S(1)} async-done(((f32[16,2,128,128]{3,2,1,0:T(8,128)}), f32[16,2,128,128]{3,2,1,0:T(8,128)S(1)}, u32[]{:S(2)}, u32[]{:S(2)}) %all-to-all-start) | async-done | bytes 2097184 | tf_op jit(solution)/shard_map/all_to_all | solution.py:299
  151.7 11.3 %all-to-all-start.1 = ((f32[16,2,128,128]{3,2,1,0:T(8,128)}), f32[16,2,128,128]{3,2,1,0:T(8,128)}, u32[]{:S(2)}, u32[]{:S(2)}) async-start(f32[16,2,128,128]{3,2,1,0:T(8,128)} %bitcast.72), calls=%async_computation.1 | async-start | bytes 4194304 | tf_op jit(solution)/shard_map/all_to_all | solution.py:299
  163.0 0.8 compare_reduce_fusion.2
  168.7 0.7 fusion.21
  171.9 0.9 slice.49
  172.8 1.0 select_bitcast_fusion.5
  173.9 2.2 dynamic-slice_select_fusion.1
  176.0 2.3 dynamic-slice_select_fusion.3
  178.3 1.1 fusion
  179.5 0.6 gather_fusion.2
  180.0 135.4 %all-reduce.3.cloned.1.call-done = f32[256,256]{1,0:T(8,128)} async-done(((f32[256,256]{1,0:T(8,128)}), f32[256,256]{1,0:T(8,128)}) %all-reduce.3.cloned.1.call-update) | async-done | bytes 262160 | tf_op jit(solution)/shard_map/psum | solution.py:322
  315.5 1.5 collective-permute-start.9
  316.9 0.6 collective-permute-start.8
  317.6 0.6 gather_fusion
  318.2 0.6 gather_fusion.1
  319.5 1.7 fusion.33
  321.2 25.5 %invert.3.inv_ref = f32[256,256]{1,0:T(8,128)} custom-call(f32[256,128]{1,0:T(8,128)} %get-tuple-element.47.left_ref, f32[256,128]{1,0:T(8,128)} %get-tuple-element.46.right_ref), custom_call_target="tpu_custom_call" | custom-call | flops 10000000000 | bytes 100000000 | tf_op jit(solution)/shard_map/invert/pallas_call | solution.py:100
  346.7 60.4 %collective-permute-done.8 = f32[16,2,128,128]{3,2,1,0:T(8,128)} collective-permute-done((f32[16,2,128,128]{3,2,1,0:T(8,128)}, f32[16,2,128,128]{3,2,1,0:T(8,128)}, u32[]{:S(2)}, u32[]{:S(2)}) %collective-permute-start.8) | collective-permute-done | bytes 2097184 | tf_op jit(solution)/shard_map/ppermute | solution.py:332
  407.1 16.1 %assemble.1.a_ref = f32[2048,1024]{1,0:T(8,128)} custom-call(s32[64]{0:T(128)S(1)} %reshape.391.rfrom, s32[64]{0:T(128)S(1)} %reshape.394.rok, s32[16]{0:T(128)S(1)} %reshape.395.cfrom, s32[16]{0:T(128)S(1)} %reshape.396.cok, f32[16384,128]{1,0:T(8,128)} %bitcast.71, f32[4,8,128,128]{3,2,1,0:T(8,128)} %bitcast.25.refs_0_, f32[4,8,128,128]{3,2,1,0:T(8,128)S(1)} %bitcast.63, ...), custom_call_target="tpu_custom_call" | custom-call | tf_op jit(solution)/shard_map/assemble/pallas_call | solution.py:164
  423.2 1.3 slice.71
  424.5 3.1 collective-permute-start.15
  427.6 2.1 fusion.32
  429.7 3.4 collective-permute-start.10
  433.1 2.9 collective-permute-start.12
  436.0 5.9 %collective-permute-done.10 = f32[1024,128]{1,0:T(8,128)S(1)} collective-permute-done((f32[1024,128]{1,0:T(8,128)}, f32[1024,128]{1,0:T(8,128)S(1)}, u32[]{:S(2)}, u32[]{:S(2)}) %collective-permute-start.10) | collective-permute-done | bytes 524320 | tf_op jit(solution)/shard_map/ppermute | solution.py:39
  442.0 1.0 collective-permute-done.12
  443.0 1.3 broadcast_select_fusion.7
  444.3 4.7 collective-permute-start.11
  449.0 1.6 collective-permute-start.13
  450.6 1.4 broadcast_select_fusion.2
  451.9 2.8 collective-permute-start.16
  454.8 1.0 collective-permute-done.11
  455.8 1.5 collective-permute-done.13
  457.4 1.1 pad_maximum_fusion
  458.6 13.8 %collective-permute-done.16 = f32[256,1024]{1,0:T(8,128)} collective-permute-done((f32[256,1024]{1,0:T(8,128)S(1)}, f32[256,1024]{1,0:T(8,128)}, u32[]{:S(2)}, u32[]{:S(2)}) %collective-permute-start.16) | collective-permute-done | bytes 1048608 | tf_op jit(solution)/shard_map/ppermute | solution.py:39
  472.7 3.4 copy-done
  476.1 15.2 %update.1 = f32[16384,128]{1,0:T(8,128)} custom-call(s32[2]{0:T(128)S(1)} %pad_add_fusion.place, f32[2048,1024]{1,0:T(8,128)S(1)} %copy-done, f32[2048,128]{1,0:T(8,128)S(1)} %get-tuple-element.41.p0_ref, f32[2048,128]{1,0:T(8,128)S(1)} %get-tuple-element.40.p1_ref, f32[256,256]{1,0:T(8,128)S(1)} %copy-done.1, f32[256,1024]{1,0:T(8,128)S(1)} %broadcast_select_fusion.4.top_ref), custom_call_target="tpu_custom_call" | custom-call | tf_op jit(solution)/shard_map/update/pallas_call | solution.py:207
  (57 shorter events, 2.0 us)
Async XLA Ops:
  7.2 16.0 %copy-start.3 = (s32[2,30]{1,0:T(2,128)S(1)}, s32[2,30]{1,0:T(2,128)}, u32[]{:S(2)}) copy-start(s32[2,30]{1,0:T(2,128)} %param.5) | copy-start | bytes 724
  8.2 15.8 %collective-permute-start.2 = (f32[256,256]{1,0:T(8,128)S(1)}, f32[256,256]{1,0:T(8,128)}, u32[]{:S(2)}, u32[]{:S(2)}) collective-permute-start(f32[256,256]{1,0:T(8,128)S(1)} %slice.66), channel_id=1, source_target_pairs={{0,8},{1,9},{2,10},{3,11},{16,24},{17,25},{18,26},{19,27}} | collective-permute-start | bytes 786440 | tf_op jit(solution)/shard_map/ppermute | solution.py:39
  16.1 41.2 %collective-permute-start.6 = (f32[256,1024]{1,0:T(8,128)S(1)}, f32[256,1024]{1,0:T(8,128)}, u32[]{:S(2)}, u32[]{:S(2)}) collective-permute-start(f32[256,1024]{1,0:T(8,128)S(1)} %slice_bitcast_fusion), channel_id=1, source_target_pairs={{0,8},{1,9},{2,10},{3,11},{16,24},{17,25},{18,26},{19,27}} | collective-permute-start | bytes 3145736 | tf_op jit(solution)/shard_map/ppermute | solution.py:39
  19.7 44.5 %collective-permute-start = (f32[1024,256]{1,0:T(8,128)S(1)}, f32[1024,256]{1,0:T(8,128)S(1)}, u32[]{:S(2)}, u32[]{:S(2)}) collective-permute-start(f32[1024,256]{1,0:T(8,128)S(1)} %slice.65), channel_id=1, source_target_pairs={{0,2},{4,6},{8,10},{12,14},{16,18},{20,22},{24,26},{28,30}} | collective-permute-start | bytes 3145736 | tf_op jit(solution)/shard_map/ppermute | solution.py:39
  24.9 2.0 copy-start.2
  25.0 22.8 %collective-permute-start.3 = (f32[256,256]{1,0:T(8,128)S(1)}, f32[256,256]{1,0:T(8,128)}, u32[]{:S(2)}, u32[]{:S(2)}) collective-permute-start(f32[256,256]{1,0:T(8,128)S(1)} %broadcast_select_fusion.10), channel_id=1, source_target_pairs={{0,4},{8,12},{1,5},{9,13},{2,6},{10,14},{3,7},{11,15},{16,20},{24,... | collective-permute-start | bytes 786440 | tf_op jit(solution)/shard_map/ppermute | solution.py:39
  48.7 7.3 %collective-permute-start.4 = (f32[256,256]{1,0:T(8,128)S(1)}, f32[256,256]{1,0:T(8,128)}, u32[]{:S(2)}, u32[]{:S(2)}) collective-permute-start(f32[256,256]{1,0:T(8,128)S(1)} %broadcast_select_fusion.11), channel_id=1, source_target_pairs={{0,2},{4,6},{8,10},{12,14},{16,18},{20,22},{24,26},{28,30}} | collective-permute-start | bytes 786440 | tf_op jit(solution)/shard_map/ppermute | solution.py:39
  56.0 9.6 %collective-permute-start.5 = (f32[256,256]{1,0:T(8,128)S(1)}, f32[256,256]{1,0:T(8,128)S(1)}, u32[]{:S(2)}, u32[]{:S(2)}) collective-permute-start(f32[256,256]{1,0:T(8,128)S(1)} %broadcast_select_fusion.12), channel_id=1, source_target_pairs={{0,1},{2,3},{4,5},{6,7},{8,9},{10,11},{12,13},{14,15},{16,17},{18,... | collective-permute-start | bytes 786440 | tf_op jit(solution)/shard_map/ppermute | solution.py:39
  58.7 34.5 %collective-permute-start.7 = (f32[256,1024]{1,0:T(8,128)S(1)}, f32[256,1024]{1,0:T(8,128)}, u32[]{:S(2)}, u32[]{:S(2)}) collective-permute-start(f32[256,1024]{1,0:T(8,128)S(1)} %broadcast_select_fusion.3), channel_id=1, source_target_pairs={{0,4},{8,12},{1,5},{9,13},{2,6},{10,14},{3,7},{11,15},{16,20},{24,... | collective-permute-start | bytes 3145736 | tf_op jit(solution)/shard_map/ppermute | solution.py:39
  66.4 29.9 %collective-permute-start.1 = (f32[1024,256]{1,0:T(8,128)S(1)}, f32[1024,256]{1,0:T(8,128)S(1)}, u32[]{:S(2)}, u32[]{:S(2)}) collective-permute-start(f32[1024,256]{1,0:T(8,128)S(1)} %broadcast_select_fusion.5), channel_id=1, source_target_pairs={{0,1},{2,3},{4,5},{6,7},{8,9},{10,11},{12,13},{14,15},{16,17},{18,... | collective-permute-start | bytes 3145736 | tf_op jit(solution)/shard_map/ppermute | solution.py:39
  105.7 46.0 %all-to-all-start = ((f32[16,2,128,128]{3,2,1,0:T(8,128)}), f32[16,2,128,128]{3,2,1,0:T(8,128)S(1)}, u32[]{:S(2)}, u32[]{:S(2)}) async-start(f32[16,2,128,128]{3,2,1,0:T(8,128)} %bitcast.73), calls=%async_computation | async-start | bytes 4194304 | tf_op jit(solution)/shard_map/all_to_all | solution.py:299
  151.7 165.3 %all-to-all-start.1 = ((f32[16,2,128,128]{3,2,1,0:T(8,128)}), f32[16,2,128,128]{3,2,1,0:T(8,128)}, u32[]{:S(2)}, u32[]{:S(2)}) async-start(f32[16,2,128,128]{3,2,1,0:T(8,128)} %bitcast.72), calls=%async_computation.1 | async-start | bytes 4194304 | tf_op jit(solution)/shard_map/all_to_all | solution.py:299
  163.0 152.5 %all-reduce.3.cloned.1.call-start = ((), (), s32[]{:S(2)}) async-start(), calls=%async_computation.2 | async-start | bytes 524288 | tf_op jit(solution)/shard_map/psum | solution.py:322
  315.5 91.6 %collective-permute-start.9 = (f32[16,2,128,128]{3,2,1,0:T(8,128)S(1)}, f32[16,2,128,128]{3,2,1,0:T(8,128)}, u32[]{:S(2)}, u32[]{:S(2)}) collective-permute-start(f32[16,2,128,128]{3,2,1,0:T(8,128)S(1)} %all-to-all-done), channel_id=1, source_target_pairs={{0,16},{16,0},{1,17},{17,1},{2,18},{18,2},{3,19},{19,3},{4,20},{20... | collective-permute-start | bytes 6291464 | tf_op jit(solution)/shard_map/ppermute | solution.py:332
  316.9 90.2 %collective-permute-start.8 = (f32[16,2,128,128]{3,2,1,0:T(8,128)}, f32[16,2,128,128]{3,2,1,0:T(8,128)}, u32[]{:S(2)}, u32[]{:S(2)}) collective-permute-start(f32[16,2,128,128]{3,2,1,0:T(8,128)} %all-to-all-done.1), channel_id=1, source_target_pairs={{0,16},{16,0},{1,17},{17,1},{2,18},{18,2},{3,19},{19,3},{4,20},{20... | collective-permute-start | bytes 6291464 | tf_op jit(solution)/shard_map/ppermute | solution.py:332
  424.5 26.0 %collective-permute-start.15 = (f32[256,1024]{1,0:T(8,128)S(1)}, f32[256,1024]{1,0:T(8,128)S(1)}, u32[]{:S(2)}, u32[]{:S(2)}) collective-permute-start(f32[256,1024]{1,0:T(8,128)S(1)} %slice.71), channel_id=1, source_target_pairs={{0,8},{1,9},{2,10},{3,11},{16,24},{17,25},{18,26},{19,27}} | collective-permute-start | bytes 3145736 | tf_op jit(solution)/shard_map/ppermute | solution.py:39
  429.7 12.3 %collective-permute-start.10 = (f32[1024,128]{1,0:T(8,128)}, f32[1024,128]{1,0:T(8,128)S(1)}, u32[]{:S(2)}, u32[]{:S(2)}) collective-permute-start(f32[1024,128]{1,0:T(8,128)} %get-tuple-element.34), channel_id=1, source_target_pairs={{0,2},{1,3},{4,6},{5,7},{8,10},{9,11},{12,14},{13,15},{16,18},{17,... | collective-permute-start | bytes 1572872 | tf_op jit(solution)/shard_map/ppermute | solution.py:39
  433.1 9.9 %collective-permute-start.12 = (f32[1024,128]{1,0:T(8,128)S(1)}, f32[1024,128]{1,0:T(8,128)}, u32[]{:S(2)}, u32[]{:S(2)}) collective-permute-start(f32[1024,128]{1,0:T(8,128)S(1)} %get-tuple-element.35), channel_id=1, source_target_pairs={{0,16},{1,17},{2,18},{3,19},{4,20},{5,21},{6,22},{7,23},{8,24},{9,... | collective-permute-start | bytes 1572872 | tf_op jit(solution)/shard_map/ppermute | solution.py:39
  444.3 11.5 %collective-permute-start.11 = (f32[1024,128]{1,0:T(8,128)S(1)}, f32[1024,128]{1,0:T(8,128)S(1)}, u32[]{:S(2)}, u32[]{:S(2)}) collective-permute-start(f32[1024,128]{1,0:T(8,128)S(1)} %get-tuple-element.32), channel_id=1, source_target_pairs={{0,16},{1,17},{2,18},{3,19},{4,20},{5,21},{6,22},{7,23},{8,24},{9,... | collective-permute-start | bytes 1572872 | tf_op jit(solution)/shard_map/ppermute | solution.py:39
  449.0 8.4 %collective-permute-start.13 = (f32[1024,128]{1,0:T(8,128)S(1)}, f32[1024,128]{1,0:T(8,128)S(1)}, u32[]{:S(2)}, u32[]{:S(2)}) collective-permute-start(f32[1024,128]{1,0:T(8,128)S(1)} %get-tuple-element.33), channel_id=1, source_target_pairs={{0,2},{1,3},{4,6},{5,7},{8,10},{9,11},{12,14},{13,15},{16,18},{17,... | collective-permute-start | bytes 1572872 | tf_op jit(solution)/shard_map/ppermute | solution.py:39
  451.9 20.4 %collective-permute-start.16 = (f32[256,1024]{1,0:T(8,128)S(1)}, f32[256,1024]{1,0:T(8,128)}, u32[]{:S(2)}, u32[]{:S(2)}) collective-permute-start(f32[256,1024]{1,0:T(8,128)S(1)} %broadcast_select_fusion.2), channel_id=1, source_target_pairs={{0,4},{8,12},{1,5},{9,13},{2,6},{10,14},{3,7},{11,15},{16,20},{24,... | collective-permute-start | bytes 3145736 | tf_op jit(solution)/shard_map/ppermute | solution.py:39
  458.5 14.2 %copy-start.1 = (f32[256,256]{1,0:T(8,128)S(1)}, f32[256,256]{1,0:T(8,128)}, u32[]{:S(2)}) copy-start(f32[256,256]{1,0:T(8,128)} %invert.3.inv_ref) | copy-start | bytes 786436
  458.5 14.1 %collective-permute-start.14 = (f32[2048,128]{1,0:T(8,128)}, f32[2048,128]{1,0:T(8,128)S(1)}, u32[]{:S(2)}, u32[]{:S(2)}) collective-permute-start(f32[2048,128]{1,0:T(8,128)} %pad_maximum_fusion), channel_id=1, source_target_pairs={{0,1},{1,0},{2,3},{3,2},{4,5},{5,4},{6,7},{7,6},{8,9},{9,8},{10,11... | collective-permute-start | bytes 3145736 | tf_op jit(solution)/shard_map/ppermute | solution.py:49
  472.7 3.4 copy-start
Sparse Core Ops, SparseCore 0:
  179.6 135.8 all-reduce.2

commit v4 on v3

--- a/solution.py
+++ b/solution.py
@@ -249,8 +249,11 @@
     lead = PANEL // BLOCK
 
     corner = spread(spread(front[:PANEL, :PANEL], "row", 1), "col", 1)
-    top_rows = spread(front[:PANEL, :], "row", 1)
-    panel_rows = spread(front[:, :PANEL], "col", 1)
+    corner, panel_rows, top_rows = lax.optimization_barrier(
+        (corner, front[:, :PANEL], front[:PANEL, :])
+    )
+    panel_rows = spread(panel_rows, "col", 1)
+    top_rows = spread(top_rows, "row", 1)
     inverse = lower_inverse(corner[:, :BLOCK], corner[:, BLOCK:])
 
     padded = jnp.concatenate([jnp.full((leaves, lead), -1, jnp.int32), block_map], axis=1)
@@ -298,31 +301,6 @@
         out = out.reshape(grid_rows * grid_cols, capacity, BLOCK, BLOCK)
         got = lax.all_to_all(out, ("row", "col"), split_axis=0, concat_axis=0, tiled=True)
         own.append(got)
-    own_map = maps[leaf_id]
-    device = leaf_id * grid_cols + col_id
-
-    def place_of(group_id, block):
-        found = own_map[group_id] == block
-        return jnp.sum(jnp.where(found, positions, 0)), jnp.any(found)
-
-    rows_at = [place_of(row_id, block) for block in range(lead)]
-    cols_at = [place_of(col_id, block) for block in range(lead)]
-
-    def cut(x, i, j, shape, ok):
-        return jnp.where(ok, lax.dynamic_slice(x, (i * BLOCK, j * BLOCK), shape), 0.0)
-
-    square = (BLOCK, BLOCK)
-    share = jnp.block([[cut(front, i, j, square, a & b) for j, b in cols_at] for i, a in rows_at])
-    left = jnp.concatenate([cut(factor, i, 0, (BLOCK, PANEL), a) for i, a in rows_at], axis=0)
-    right = jnp.concatenate([cut(upper, 0, j, (PANEL, BLOCK), b) for j, b in cols_at], axis=1)
-    first = parent_front[:PANEL, 0, 0, :]
-    given = jnp.concatenate(
-        [jnp.where((row_id == 0) & (device == block), first, 0.0) for block in range(lead)], axis=1
-    )
-    corner_parent = lax.psum(given + (share - dot(left, right)), ("leaf", "row", "col"))
-    corner_parent, own[-1] = lax.optimization_barrier((corner_parent, own[-1]))
-    inverse_parent = lower_inverse(corner_parent[:, :BLOCK], corner_parent[:, BLOCK:])
-
     pieces = [[] for _ in range(leaves)]
     for got in own:
         for shift in range(leaves):
@@ -334,19 +312,22 @@
                 moved.reshape(grid_rows, grid_cols * capacity, BLOCK, BLOCK)
             )
     pieces = [x for part in pieces for x in part]
-    inverse_parent, rok = lax.optimization_barrier((inverse_parent, rok))
     assembled = assemble(
         parent_front.reshape(parent_rows * kblocks, BLOCK),
         pieces, leaves, capacity, kblocks, rfrom, rok, cfrom, cok,
     )
 
-    panel = assembled[:, :BLOCK]
+    piece = spread(spread(assembled[:PANEL, :BLOCK], "col", 2), "leaf", 1)
+    piece, panel = lax.optimization_barrier((piece, assembled[:, :BLOCK]))
     middle = parent_rows // 2
     upper_half = spread(spread(panel[:middle], "col", 2), "leaf", 1)
     lower_half = spread(spread(panel[middle:], "leaf", 1), "col", 2)
-    top = spread(assembled[:PANEL], "row", 1)
     panel0, panel1 = swap_pairs(jnp.concatenate([upper_half, lower_half], axis=0))
-    place = jnp.stack([row_id, device]).astype(jnp.int32)
+    corner0, corner1 = swap_pairs(spread(piece, "row", 1))
+    corner0, corner1, top = lax.optimization_barrier((corner0, corner1, assembled[:PANEL]))
+    top = spread(top, "row", 1)
+    inverse_parent = lower_inverse(corner0, corner1)
+    place = jnp.stack([row_id, leaf_id * grid_cols + col_id]).astype(jnp.int32)
     result = update(assembled, panel0, panel1, inverse_parent, top, place, kblocks)
     return factor[None], result.reshape(parent_front.shape)
 

time: 501 us -> 383 us (0.76)
  waiting for transfers between devices: 276 us -> 177 us
  between operations: 21.8 us -> 1.12 us
  starting transfers between devices: 63.5 us -> 78.6 us
  other arithmetic: 17.1 us -> 7.54 us
    psum x1 -> x0, waiting for transfers between devices: 135 us -> none  [per_device(): lax.psum(given + (share - dot(left, right)), ('leaf', 'row', 'col'))]
    all_to_all x2, waiting for transfers between devices: 34.7 us -> 74.2 us  [per_device(): lax.all_to_all(out, ('row', 'col'), split_axis=0, concat_axis=0, tiled=True)]
    ppermute x14 -> x18, starting transfers between devices: 45.2 us -> 59.4 us  [spread(): got = lax.ppermute(x, axis, pairs)]
    ppermute x2, waiting for transfers between devices: 60.4 us -> 47.7 us  [per_device(): moved = lax.ppermute(got, 'leaf', pairs)]
    ppermute x14 -> x18, waiting for transfers between devices: 45.8 us -> 55.2 us  [spread(): got = lax.ppermute(x, axis, pairs)]
    select_n x4 -> x0, other arithmetic: 5.47 us -> none  [the longest x3 5.45 us: cut(): jnp.where(ok, lax.dynamic_slice(x, (i * BLOCK, j * BLOCK), shape), 0.0)]
  transfers between devices with their start and end apart: 20 -> 24, of which waited for: 10 -> 15; matrix products, arithmetic and copies ran while one was open for 7% -> 5% of each run, Pallas kernels for 12% -> 15%
where the time goes in v4:
time: 383 us; the launch traced here: 381 us
  waiting for transfers between devices  177 us (46%)
  Pallas kernels  95.3 us (25%)
  starting transfers between devices  78.6 us (21%)
  local copies, waits for them, and re-layouts  15.5 us (4%)
  other arithmetic  7.54 us (2%)
  matrix products  5.92 us (2%)
    all_to_all x2, waiting for transfers between devices, per_device(): lax.all_to_all(out, ('row', 'col'), split_axis=0, concat_axis=0, tiled=True)  74.2 us
    ppermute x18, starting transfers between devices, spread(): got = lax.ppermute(x, axis, pairs)  59.4 us
    ppermute x18, waiting for transfers between devices, spread(): got = lax.ppermute(x, axis, pairs)  55.2 us
    pallas_call x2, Pallas kernels, lower_inverse(): pl.pallas_call(invert_kernel, out_shape=jax.ShapeDtypeStruct((PANEL, PANE...  51.1 us
    ppermute x2, waiting for transfers between devices, per_device(): moved = lax.ppermute(got, 'leaf', pairs)  47.7 us
    pallas_call x1, Pallas kernels, assemble(): pl.pallas_call(functools.partial(assemble_kernel, leaves, capacity, kbloc...  16.3 us
    all_to_all x2, starting transfers between devices, per_device(): lax.all_to_all(out, ('row', 'col'), split_axis=0, concat_axis=0, tiled=True)  16 us
    pallas_call x1, Pallas kernels, update(): pl.pallas_call(functools.partial(update_kernel, kblocks, PANEL // BLOCK),...  15 us
  transfers between devices with their start and end apart: 24, of which 15 were waited for; matrix products, arithmetic and copies ran while one was open for 5% of the time, Pallas kernels for 15%

profile of v4, /device:TPU:0, one launch (start us, length us, event | category | flops | bytes accessed | tf_op | source)
XLA Modules:
  0.0 381.1 jit_solution(2963890789050648056)
XLA Ops:
  0.6 1.0 slice.58
  1.6 6.0 %collective-permute-start = (f32[256,256]{1,0:T(8,128)S(1)}, f32[256,256]{1,0:T(8,128)S(1)}, u32[]{:S(2)}, u32[]{:S(2)}) collective-permute-start(f32[256,256]{1,0:T(8,128)S(1)} %slice.58), channel_id=1, source_target_pairs={{0,8},{1,9},{2,10},{3,11},{16,24},{17,25},{18,26},{19,27}} | collective-permute-start | bytes 786440 | tf_op jit(solution)/shard_map/ppermute | solution.py:39
  7.6 0.8 concatenate.6
  8.9 4.2 %collective-permute-done = f32[256,256]{1,0:T(8,128)S(1)} collective-permute-done((f32[256,256]{1,0:T(8,128)S(1)}, f32[256,256]{1,0:T(8,128)S(1)}, u32[]{:S(2)}, u32[]{:S(2)}) %collective-permute-start) | collective-permute-done | bytes 262176 | tf_op jit(solution)/shard_map/ppermute | solution.py:39
  13.1 1.0 broadcast_select_fusion.10
  14.1 1.3 collective-permute-start.1
  15.4 4.9 %collective-permute-done.1 = f32[256,256]{1,0:T(8,128)S(1)} collective-permute-done((f32[256,256]{1,0:T(8,128)S(1)}, f32[256,256]{1,0:T(8,128)S(1)}, u32[]{:S(2)}, u32[]{:S(2)}) %collective-permute-start.1) | collective-permute-done | bytes 262176 | tf_op jit(solution)/shard_map/ppermute | solution.py:39
  20.4 3.4 collective-permute-start.2
  23.8 1.3 slice.59
  25.2 2.5 collective-permute-done.2
  27.7 1.3 collective-permute-start.3
  29.0 1.3 slice_bitcast_fusion
  30.4 5.4 %collective-permute-start.4 = (f32[1024,256]{1,0:T(8,128)S(1)}, f32[1024,256]{1,0:T(8,128)}, u32[]{:S(2)}, u32[]{:S(2)}) collective-permute-start(f32[1024,256]{1,0:T(8,128)S(1)} %slice.59), channel_id=1, source_target_pairs={{0,2},{4,6},{8,10},{12,14},{16,18},{20,22},{24,26},{28,30}} | collective-permute-start | bytes 3145736 | tf_op jit(solution)/shard_map/ppermute | solution.py:39
  36.0 0.7 reshape.362.col_ids
  36.7 5.3 %collective-permute-start.6 = (f32[256,1024]{1,0:T(8,128)S(1)}, f32[256,1024]{1,0:T(8,128)S(1)}, u32[]{:S(2)}, u32[]{:S(2)}) collective-permute-start(f32[256,1024]{1,0:T(8,128)S(1)} %slice_bitcast_fusion), channel_id=1, source_target_pairs={{0,8},{1,9},{2,10},{3,11},{16,24},{17,25},{18,26},{19,27}} | collective-permute-start | bytes 3145736 | tf_op jit(solution)/shard_map/ppermute | solution.py:39
  42.2 0.6 slice_bitcast_fusion.1
  42.8 0.7 fusion.21
  43.5 3.6 collective-permute-done.4
  47.2 2.3 collective-permute-start.5
  49.5 14.0 %collective-permute-done.6 = f32[256,1024]{1,0:T(8,128)S(1)} collective-permute-done((f32[256,1024]{1,0:T(8,128)S(1)}, f32[256,1024]{1,0:T(8,128)S(1)}, u32[]{:S(2)}, u32[]{:S(2)}) %collective-permute-start.6) | collective-permute-done | bytes 1048608 | tf_op jit(solution)/shard_map/ppermute | solution.py:39
  63.7 1.4 collective-permute-start.7
  65.0 25.5 %invert.2 = f32[256,256]{1,0:T(8,128)} custom-call(f32[256,128]{1,0:T(8,128)} %get-tuple-element.39.left_ref, f32[256,128]{1,0:T(8,128)} %get-tuple-element.38.right_ref), custom_call_target="tpu_custom_call" | custom-call | flops 10000000000 | bytes 100000000 | tf_op jit(solution)/shard_map/invert/pallas_call | solution.py:100
  90.6 2.9 fusion.2.f_ref
  93.5 3.0 fusion.u_ref
  96.5 6.4 %schur.2 = f32[4,8,128,128]{3,2,1,0:T(8,128)} custom-call(s32[4]{0:T(128)} %get-tuple-element.43.row_ids, s32[8]{0:T(128)} %reshape.362.col_ids, f32[1024,1024]{1,0:T(8,128)} %bitcast.36, f32[1024,256]{1,0:T(8,128)} %fusion.2.f_ref, f32[256,1024]{1,0:T(8,128)} %fusion.u_ref), custom_call_target="tpu_custom_call" | custom-call | flops 1610612736 | bytes 4194304 | tf_op jit(solution)/shard_map/schur/pallas_call | solution.py:119
  102.9 4.8 %all-to-all-start = ((f32[16,2,128,128]{3,2,1,0:T(8,128)}), f32[16,2,128,128]{3,2,1,0:T(8,128)S(1)}, u32[]{:S(2)}, u32[]{:S(2)}) async-start(f32[16,2,128,128]{3,2,1,0:T(8,128)} %bitcast.41), calls=%async_computation | async-start | bytes 4194304 | tf_op jit(solution)/shard_map/all_to_all | solution.py:302
  107.7 6.5 %schur.3 = f32[4,8,128,128]{3,2,1,0:T(8,128)} custom-call(s32[4]{0:T(128)} %get-tuple-element.42.row_ids, s32[8]{0:T(128)} %reshape.362.col_ids, f32[1024,1024]{1,0:T(8,128)} %bitcast.37, f32[1024,256]{1,0:T(8,128)} %fusion.2.f_ref, f32[256,1024]{1,0:T(8,128)} %fusion.u_ref), custom_call_target="tpu_custom_call" | custom-call | flops 1610612736 | bytes 4194304 | tf_op jit(solution)/shard_map/schur/pallas_call | solution.py:119
  114.2 34.6 %all-to-all-done = f32[16,2,128,128]{3,2,1,0:T(8,128)S(1)} async-done(((f32[16,2,128,128]{3,2,1,0:T(8,128)}), f32[16,2,128,128]{3,2,1,0:T(8,128)S(1)}, u32[]{:S(2)}, u32[]{:S(2)}) %all-to-all-start) | async-done | bytes 2097184 | tf_op jit(solution)/shard_map/all_to_all | solution.py:302
  148.8 11.3 %all-to-all-start.1 = ((f32[16,2,128,128]{3,2,1,0:T(8,128)}), f32[16,2,128,128]{3,2,1,0:T(8,128)}, u32[]{:S(2)}, u32[]{:S(2)}) async-start(f32[16,2,128,128]{3,2,1,0:T(8,128)} %bitcast.40), calls=%async_computation.1 | async-start | bytes 4194304 | tf_op jit(solution)/shard_map/all_to_all | solution.py:302
  160.1 1.6 collective-permute-start.8
  161.7 39.6 %all-to-all-done.1 = f32[16,2,128,128]{3,2,1,0:T(8,128)} async-done(((f32[16,2,128,128]{3,2,1,0:T(8,128)}), f32[16,2,128,128]{3,2,1,0:T(8,128)}, u32[]{:S(2)}, u32[]{:S(2)}) %all-to-all-start.1) | async-done | bytes 2097184 | tf_op jit(solution)/shard_map/all_to_all | solution.py:302
  201.3 1.5 collective-permute-start.9
  202.8 0.6 gather_fusion
  203.4 0.6 gather_fusion.2
  203.9 0.6 gather_fusion.1
  205.3 3.4 collective-permute-done.8
  208.7 44.3 %collective-permute-done.9 = f32[16,2,128,128]{3,2,1,0:T(8,128)} collective-permute-done((f32[16,2,128,128]{3,2,1,0:T(8,128)}, f32[16,2,128,128]{3,2,1,0:T(8,128)}, u32[]{:S(2)}, u32[]{:S(2)}) %collective-permute-start.9) | collective-permute-done | bytes 2097184 | tf_op jit(solution)/shard_map/ppermute | solution.py:310
  253.0 16.3 %assemble.1.a_ref = f32[2048,1024]{1,0:T(8,128)} custom-call(s32[64]{0:T(128)S(1)} %reshape.357.rfrom, s32[64]{0:T(128)S(1)} %reshape.358.rok, s32[16]{0:T(128)S(1)} %reshape.359.cfrom, s32[16]{0:T(128)S(1)} %reshape.360.cok, f32[16384,128]{1,0:T(8,128)} %bitcast.39, f32[4,8,128,128]{3,2,1,0:T(8,128)S(1)} %bitcast.32, f32[4,8,128,128]{3,2,1,0:T(8,128)} %bitcast.16.refs_1_, ...), custom_call_target="tpu_custom_call" | custom-call | tf_op jit(solution)/shard_map/assemble/pallas_call | solution.py:164
  269.4 0.9 slice.60
  270.3 3.6 collective-permute-start.10
  273.9 2.5 collective-permute-done.10
  276.4 0.9 broadcast_select_fusion.18
  277.3 3.2 collective-permute-start.11
  280.5 1.3 slice.61
  281.8 1.2 collective-permute-done.11
  283.0 5.2 %collective-permute-start.17 = (f32[256,128]{1,0:T(8,128)S(1)}, f32[256,128]{1,0:T(8,128)S(1)}, u32[]{:S(2)}, u32[]{:S(2)}) collective-permute-start(f32[256,128]{1,0:T(8,128)S(1)} %broadcast_select_fusion.19), channel_id=1, source_target_pairs={{0,8},{1,9},{2,10},{3,11},{16,24},{17,25},{18,26},{19,27}} | collective-permute-start | bytes 393224 | tf_op jit(solution)/shard_map/ppermute | solution.py:39
  288.3 4.4 %collective-permute-start.12 = (f32[1024,128]{1,0:T(8,128)S(1)}, f32[1024,128]{1,0:T(8,128)S(1)}, u32[]{:S(2)}, u32[]{:S(2)}) collective-permute-start(f32[1024,128]{1,0:T(8,128)S(1)} %get-tuple-element.34), channel_id=1, source_target_pairs={{0,2},{1,3},{4,6},{5,7},{8,10},{9,11},{12,14},{13,15},{16,18},{17,... | collective-permute-start | bytes 1572872 | tf_op jit(solution)/shard_map/ppermute | solution.py:39
  292.7 4.4 %collective-permute-start.14 = (f32[1024,128]{1,0:T(8,128)S(1)}, f32[1024,128]{1,0:T(8,128)S(1)}, u32[]{:S(2)}, u32[]{:S(2)}) collective-permute-start(f32[1024,128]{1,0:T(8,128)S(1)} %get-tuple-element.35), channel_id=1, source_target_pairs={{0,16},{1,17},{2,18},{3,19},{4,20},{5,21},{6,22},{7,23},{8,24},{9,... | collective-permute-start | bytes 1572872 | tf_op jit(solution)/shard_map/ppermute | solution.py:39
  297.1 1.9 collective-permute-start.18
  299.0 2.5 collective-permute-done.18
  301.6 2.9 collective-permute-done.14
  304.7 4.4 %collective-permute-start.13 = (f32[1024,128]{1,0:T(8,128)S(1)}, f32[1024,128]{1,0:T(8,128)S(1)}, u32[]{:S(2)}, u32[]{:S(2)}) collective-permute-start(f32[1024,128]{1,0:T(8,128)S(1)} %get-tuple-element.32), channel_id=1, source_target_pairs={{0,16},{1,17},{2,18},{3,19},{4,20},{5,21},{6,22},{7,23},{8,24},{9,... | collective-permute-start | bytes 1572872 | tf_op jit(solution)/shard_map/ppermute | solution.py:39
  309.1 1.3 slice.62
  310.4 0.7 broadcast_select_fusion.16
  311.1 2.3 collective-permute-start.20
  313.5 2.4 collective-permute-start.15
  316.0 7.1 %collective-permute-done.15 = f32[1024,128]{1,0:T(8,128)} collective-permute-done((f32[1024,128]{1,0:T(8,128)S(1)}, f32[1024,128]{1,0:T(8,128)}, u32[]{:S(2)}, u32[]{:S(2)}) %collective-permute-start.15) | collective-permute-done | bytes 524320 | tf_op jit(solution)/shard_map/ppermute | solution.py:39
  323.2 1.1 pad_maximum_fusion
  324.2 9.8 %collective-permute-done.20 = f32[256,1024]{1,0:T(8,128)} collective-permute-done((f32[256,1024]{1,0:T(8,128)S(1)}, f32[256,1024]{1,0:T(8,128)}, u32[]{:S(2)}, u32[]{:S(2)}) %collective-permute-start.20) | collective-permute-done | bytes 1048608 | tf_op jit(solution)/shard_map/ppermute | solution.py:39
  334.2 1.4 collective-permute-start.21
  335.6 25.6 %invert.3.inv_ref = f32[256,256]{1,0:T(8,128)} custom-call(f32[256,128]{1,0:T(8,128)} %get-tuple-element.15.left_ref, f32[256,128]{1,0:T(8,128)} %get-tuple-element.16.right_ref), custom_call_target="tpu_custom_call" | custom-call | flops 10000000000 | bytes 100000000 | tf_op jit(solution)/shard_map/invert/pallas_call | solution.py:100
  361.2 1.4 broadcast_select_fusion
  362.8 3.4 copy-done
  366.1 15.0 %update.1 = f32[16384,128]{1,0:T(8,128)} custom-call(s32[2]{0:T(128)S(1)} %pad_add_fusion.place, f32[2048,1024]{1,0:T(8,128)S(1)} %copy-done, f32[2048,128]{1,0:T(8,128)S(1)} %get-tuple-element.31.p0_ref, f32[2048,128]{1,0:T(8,128)S(1)} %get-tuple-element.30.p1_ref, f32[256,256]{1,0:T(8,128)S(1)} %copy-done.1, f32[256,1024]{1,0:T(8,128)S(1)} %broadcast_select_fusion.4.top_ref), custom_call_target="tpu_custom_call" | custom-call | tf_op jit(solution)/shard_map/update/pallas_call | solution.py:207
  (57 shorter events, 3.2 us)
Async XLA Ops:
  1.6 11.5 %collective-permute-start = (f32[256,256]{1,0:T(8,128)S(1)}, f32[256,256]{1,0:T(8,128)S(1)}, u32[]{:S(2)}, u32[]{:S(2)}) collective-permute-start(f32[256,256]{1,0:T(8,128)S(1)} %slice.58), channel_id=1, source_target_pairs={{0,8},{1,9},{2,10},{3,11},{16,24},{17,25},{18,26},{19,27}} | collective-permute-start | bytes 786440 | tf_op jit(solution)/shard_map/ppermute | solution.py:39
  14.1 6.3 %collective-permute-start.1 = (f32[256,256]{1,0:T(8,128)S(1)}, f32[256,256]{1,0:T(8,128)S(1)}, u32[]{:S(2)}, u32[]{:S(2)}) collective-permute-start(f32[256,256]{1,0:T(8,128)S(1)} %broadcast_select_fusion.10), channel_id=1, source_target_pairs={{0,4},{8,12},{1,5},{9,13},{2,6},{10,14},{3,7},{11,15},{16,20},{24,... | collective-permute-start | bytes 786440 | tf_op jit(solution)/shard_map/ppermute | solution.py:39
  20.4 7.3 %collective-permute-start.2 = (f32[256,256]{1,0:T(8,128)S(1)}, f32[256,256]{1,0:T(8,128)S(1)}, u32[]{:S(2)}, u32[]{:S(2)}) collective-permute-start(f32[256,256]{1,0:T(8,128)S(1)} %broadcast_select_fusion.11), channel_id=1, source_target_pairs={{0,2},{4,6},{8,10},{12,14},{16,18},{20,22},{24,26},{28,30}} | collective-permute-start | bytes 786440 | tf_op jit(solution)/shard_map/ppermute | solution.py:39
  27.7 2.6 collective-permute-start.3
  30.4 16.7 %collective-permute-start.4 = (f32[1024,256]{1,0:T(8,128)S(1)}, f32[1024,256]{1,0:T(8,128)}, u32[]{:S(2)}, u32[]{:S(2)}) collective-permute-start(f32[1024,256]{1,0:T(8,128)S(1)} %slice.59), channel_id=1, source_target_pairs={{0,2},{4,6},{8,10},{12,14},{16,18},{20,22},{24,26},{28,30}} | collective-permute-start | bytes 3145736 | tf_op jit(solution)/shard_map/ppermute | solution.py:39
  36.7 26.8 %collective-permute-start.6 = (f32[256,1024]{1,0:T(8,128)S(1)}, f32[256,1024]{1,0:T(8,128)S(1)}, u32[]{:S(2)}, u32[]{:S(2)}) collective-permute-start(f32[256,1024]{1,0:T(8,128)S(1)} %slice_bitcast_fusion), channel_id=1, source_target_pairs={{0,8},{1,9},{2,10},{3,11},{16,24},{17,25},{18,26},{19,27}} | collective-permute-start | bytes 3145736 | tf_op jit(solution)/shard_map/ppermute | solution.py:39
  47.2 43.4 %collective-permute-start.5 = (f32[1024,256]{1,0:T(8,128)S(1)}, f32[1024,256]{1,0:T(8,128)}, u32[]{:S(2)}, u32[]{:S(2)}) collective-permute-start(f32[1024,256]{1,0:T(8,128)S(1)} %broadcast_select_fusion.5), channel_id=1, source_target_pairs={{0,1},{2,3},{4,5},{6,7},{8,9},{10,11},{12,13},{14,15},{16,17},{18,... | collective-permute-start | bytes 3145736 | tf_op jit(solution)/shard_map/ppermute | solution.py:39
  63.7 29.9 %collective-permute-start.7 = (f32[256,1024]{1,0:T(8,128)S(1)}, f32[256,1024]{1,0:T(8,128)S(1)}, u32[]{:S(2)}, u32[]{:S(2)}) collective-permute-start(f32[256,1024]{1,0:T(8,128)S(1)} %broadcast_select_fusion.3), channel_id=1, source_target_pairs={{0,4},{8,12},{1,5},{9,13},{2,6},{10,14},{3,7},{11,15},{16,20},{24,... | collective-permute-start | bytes 3145736 | tf_op jit(solution)/shard_map/ppermute | solution.py:39
  102.9 45.9 %all-to-all-start = ((f32[16,2,128,128]{3,2,1,0:T(8,128)}), f32[16,2,128,128]{3,2,1,0:T(8,128)S(1)}, u32[]{:S(2)}, u32[]{:S(2)}) async-start(f32[16,2,128,128]{3,2,1,0:T(8,128)} %bitcast.41), calls=%async_computation | async-start | bytes 4194304 | tf_op jit(solution)/shard_map/all_to_all | solution.py:302
  148.8 52.4 %all-to-all-start.1 = ((f32[16,2,128,128]{3,2,1,0:T(8,128)}), f32[16,2,128,128]{3,2,1,0:T(8,128)}, u32[]{:S(2)}, u32[]{:S(2)}) async-start(f32[16,2,128,128]{3,2,1,0:T(8,128)} %bitcast.40), calls=%async_computation.1 | async-start | bytes 4194304 | tf_op jit(solution)/shard_map/all_to_all | solution.py:302
  160.1 48.6 %collective-permute-start.8 = (f32[16,2,128,128]{3,2,1,0:T(8,128)S(1)}, f32[16,2,128,128]{3,2,1,0:T(8,128)}, u32[]{:S(2)}, u32[]{:S(2)}) collective-permute-start(f32[16,2,128,128]{3,2,1,0:T(8,128)S(1)} %all-to-all-done), channel_id=1, source_target_pairs={{0,16},{16,0},{1,17},{17,1},{2,18},{18,2},{3,19},{19,3},{4,20},{20... | collective-permute-start | bytes 6291464 | tf_op jit(solution)/shard_map/ppermute | solution.py:310
  201.3 51.8 %collective-permute-start.9 = (f32[16,2,128,128]{3,2,1,0:T(8,128)}, f32[16,2,128,128]{3,2,1,0:T(8,128)}, u32[]{:S(2)}, u32[]{:S(2)}) collective-permute-start(f32[16,2,128,128]{3,2,1,0:T(8,128)} %all-to-all-done.1), channel_id=1, source_target_pairs={{0,16},{16,0},{1,17},{17,1},{2,18},{18,2},{3,19},{19,3},{4,20},{20... | collective-permute-start | bytes 6291464 | tf_op jit(solution)/shard_map/ppermute | solution.py:310
  270.3 6.1 %collective-permute-start.10 = (f32[256,128]{1,0:T(8,128)S(1)}, f32[256,128]{1,0:T(8,128)S(1)}, u32[]{:S(2)}, u32[]{:S(2)}) collective-permute-start(f32[256,128]{1,0:T(8,128)S(1)} %slice.60), channel_id=1, source_target_pairs={{0,2},{1,3},{4,6},{5,7},{8,10},{9,11},{12,14},{13,15},{16,18},{17,... | collective-permute-start | bytes 393224 | tf_op jit(solution)/shard_map/ppermute | solution.py:39
  277.3 5.7 %collective-permute-start.11 = (f32[256,128]{1,0:T(8,128)S(1)}, f32[256,128]{1,0:T(8,128)S(1)}, u32[]{:S(2)}, u32[]{:S(2)}) collective-permute-start(f32[256,128]{1,0:T(8,128)S(1)} %broadcast_select_fusion.18), channel_id=1, source_target_pairs={{0,16},{1,17},{2,18},{3,19},{4,20},{5,21},{6,22},{7,23},{8,24},{9,... | collective-permute-start | bytes 393224 | tf_op jit(solution)/shard_map/ppermute | solution.py:39
  283.0 14.1 %collective-permute-start.17 = (f32[256,128]{1,0:T(8,128)S(1)}, f32[256,128]{1,0:T(8,128)S(1)}, u32[]{:S(2)}, u32[]{:S(2)}) collective-permute-start(f32[256,128]{1,0:T(8,128)S(1)} %broadcast_select_fusion.19), channel_id=1, source_target_pairs={{0,8},{1,9},{2,10},{3,11},{16,24},{17,25},{18,26},{19,27}} | collective-permute-start | bytes 393224 | tf_op jit(solution)/shard_map/ppermute | solution.py:39
  288.3 13.3 %collective-permute-start.12 = (f32[1024,128]{1,0:T(8,128)S(1)}, f32[1024,128]{1,0:T(8,128)S(1)}, u32[]{:S(2)}, u32[]{:S(2)}) collective-permute-start(f32[1024,128]{1,0:T(8,128)S(1)} %get-tuple-element.34), channel_id=1, source_target_pairs={{0,2},{1,3},{4,6},{5,7},{8,10},{9,11},{12,14},{13,15},{16,18},{17,... | collective-permute-start | bytes 1572872 | tf_op jit(solution)/shard_map/ppermute | solution.py:39
  292.7 11.8 %collective-permute-start.14 = (f32[1024,128]{1,0:T(8,128)S(1)}, f32[1024,128]{1,0:T(8,128)S(1)}, u32[]{:S(2)}, u32[]{:S(2)}) collective-permute-start(f32[1024,128]{1,0:T(8,128)S(1)} %get-tuple-element.35), channel_id=1, source_target_pairs={{0,16},{1,17},{2,18},{3,19},{4,20},{5,21},{6,22},{7,23},{8,24},{9,... | collective-permute-start | bytes 1572872 | tf_op jit(solution)/shard_map/ppermute | solution.py:39
  297.1 4.4 %collective-permute-start.18 = (f32[256,128]{1,0:T(8,128)S(1)}, f32[256,128]{1,0:T(8,128)S(1)}, u32[]{:S(2)}, u32[]{:S(2)}) collective-permute-start(f32[256,128]{1,0:T(8,128)S(1)} %broadcast_select_fusion.14), channel_id=1, source_target_pairs={{0,4},{8,12},{1,5},{9,13},{2,6},{10,14},{3,7},{11,15},{16,20},{24,... | collective-permute-start | bytes 393224 | tf_op jit(solution)/shard_map/ppermute | solution.py:39
  301.5 8.9 %collective-permute-start.19 = (f32[256,128]{1,0:T(8,128)S(1)}, f32[256,128]{1,0:T(8,128)S(1)}, u32[]{:S(2)}, u32[]{:S(2)}) collective-permute-start(f32[256,128]{1,0:T(8,128)S(1)} %broadcast_select_fusion.15), channel_id=1, source_target_pairs={{0,1},{1,0},{2,3},{3,2},{4,5},{5,4},{6,7},{7,6},{8,9},{9,8},{10,11... | collective-permute-start | bytes 393224 | tf_op jit(solution)/shard_map/ppermute | solution.py:49
  304.7 11.2 %collective-permute-start.13 = (f32[1024,128]{1,0:T(8,128)S(1)}, f32[1024,128]{1,0:T(8,128)S(1)}, u32[]{:S(2)}, u32[]{:S(2)}) collective-permute-start(f32[1024,128]{1,0:T(8,128)S(1)} %get-tuple-element.32), channel_id=1, source_target_pairs={{0,16},{1,17},{2,18},{3,19},{4,20},{5,21},{6,22},{7,23},{8,24},{9,... | collective-permute-start | bytes 1572872 | tf_op jit(solution)/shard_map/ppermute | solution.py:39
  311.1 22.9 %collective-permute-start.20 = (f32[256,1024]{1,0:T(8,128)S(1)}, f32[256,1024]{1,0:T(8,128)}, u32[]{:S(2)}, u32[]{:S(2)}) collective-permute-start(f32[256,1024]{1,0:T(8,128)S(1)} %slice.62), channel_id=1, source_target_pairs={{0,8},{1,9},{2,10},{3,11},{16,24},{17,25},{18,26},{19,27}} | collective-permute-start | bytes 3145736 | tf_op jit(solution)/shard_map/ppermute | solution.py:39
  313.5 9.6 %collective-permute-start.15 = (f32[1024,128]{1,0:T(8,128)S(1)}, f32[1024,128]{1,0:T(8,128)}, u32[]{:S(2)}, u32[]{:S(2)}) collective-permute-start(f32[1024,128]{1,0:T(8,128)S(1)} %get-tuple-element.33), channel_id=1, source_target_pairs={{0,2},{1,3},{4,6},{5,7},{8,10},{9,11},{12,14},{13,15},{16,18},{17,... | collective-permute-start | bytes 1572872 | tf_op jit(solution)/shard_map/ppermute | solution.py:39
  324.2 36.9 %collective-permute-start.16 = (f32[2048,128]{1,0:T(8,128)}, f32[2048,128]{1,0:T(8,128)}, u32[]{:S(2)}, u32[]{:S(2)}) collective-permute-start(f32[2048,128]{1,0:T(8,128)} %pad_maximum_fusion), channel_id=1, source_target_pairs={{0,1},{1,0},{2,3},{3,2},{4,5},{5,4},{6,7},{7,6},{8,9},{9,8},{10,11... | collective-permute-start | bytes 3145736 | tf_op jit(solution)/shard_map/ppermute | solution.py:49
  334.2 28.3 %collective-permute-start.21 = (f32[256,1024]{1,0:T(8,128)S(1)}, f32[256,1024]{1,0:T(8,128)S(1)}, u32[]{:S(2)}, u32[]{:S(2)}) collective-permute-start(f32[256,1024]{1,0:T(8,128)S(1)} %broadcast_select_fusion.2), channel_id=1, source_target_pairs={{0,4},{8,12},{1,5},{9,13},{2,6},{10,14},{3,7},{11,15},{16,20},{24,... | collective-permute-start | bytes 3145736 | tf_op jit(solution)/shard_map/ppermute | solution.py:39
  361.2 1.6 copy-start.1
  362.7 3.4 copy-start
